TPU v7x, 256 devices: a whole 4x4x8 slice. The times are simulated.
256 devices in a mesh: seq: 32 (over y, z), kvh: 8 (over x, core).
Axes of the slice: x: 4, y: 4, z: 8, core: 2. Of those that a mesh axis runs over, the one named last changes fastest.
Arguments:
- queries: bfloat16 [16384, 64, 128], P('seq', 'kvh'), may hold values from -24 to 24, as said below
- keys: bfloat16 [16384, 8, 128], P('seq', 'kvh'), may hold values from -24 to 24, as said below
- values: bfloat16 [16384, 8, 128], P('seq', 'kvh'), may hold values from -6 to 6
- teacher: bfloat16 [16384, 64, 128], P('seq', 'kvh'), may hold values from -6 to 6
- q_map: bfloat16 [64, 128, 64], P('kvh'), as said below
- k_map: bfloat16 [64, 128, 64], P('kvh'), as said below
Outputs:
- attn_out: bfloat16 [16384, 64, 128], P('seq', 'kvh')
- grad_q_map: float32 [64, 128, 64], P('kvh')
- grad_k_map: float32 [64, 128, 64], P('kvh')
- loss: float32 [], replicated
Inputs may be any that keep to these rules, and one draw needn't show every extreme that they name: `queries`: Real-valued entries. `keys`: Real-valued entries. `q_map`: Real-valued entries. `k_map`: Real-valued entries.
All inputs are finite; a program needn't handle non-finite values.
Results may differ from a plain program's by a relative error of at most 0.001.
Values may be sent and summed in bfloat16 or wider, within the bound.
A program may use at most 128 MiB of HBM per device.

v0:
```python
import jax
import jax.numpy as jnp
from jax import lax
from jax.sharding import PartitionSpec as P

WIN = 64


def passed_along(value, axis, steps):
    count = lax.axis_size(axis)
    initial, last = (max(0, -steps), min(count, count - steps))
    return lax.ppermute(value, axis, [(source, source + steps) for source in range(initial, last)])


def entering(value, axis, combine, identity, reverse):
    length, here = (lax.axis_size(axis), lax.axis_index(axis))
    everything = jax.tree.map(lambda part: lax.all_gather(part, axis), value)
    start = jax.tree.map(
        lambda part, zero: jnp.broadcast_to(jnp.asarray(zero, part.dtype), part.shape),
        value,
        identity,
    )

    def hop(k, before):
        at = length - 1 - k if reverse else k
        reached = at > here if reverse else at < here
        new = combine(before, jax.tree.map(lambda part: part[at], everything))
        return jax.tree.map(lambda a, b: jnp.where(reached, a, b), new, before)

    return lax.fori_loop(0, length, hop, start)


def feature_maps(scores):
    return jnp.concatenate(
        [jax.nn.softmax(scores, axis=-1), jax.nn.softmax(-scores, axis=-1)], axis=-1
    )


def map_backward(feats, grad_feats):
    half = feats.shape[-1] // 2
    upper = feats[..., :half]
    lower = feats[..., half:]
    grad_up = grad_feats[..., :half]
    grad_low = grad_feats[..., half:]
    first = upper * (grad_up - jnp.sum(upper * grad_up, axis=-1, keepdims=True))
    second = lower * (grad_low - jnp.sum(lower * grad_low, axis=-1, keepdims=True))
    return first - second


def hdot(left, right):
    return jnp.dot(left, right, precision=lax.Precision.HIGHEST, preferred_element_type=jnp.float32)


def add_pair(earlier, later):
    return (earlier[0] + later[0], earlier[1] + later[1])


def body(queries, keys, values, teacher, q_map, k_map):
    tok, heads, width = queries.shape
    kv_heads = keys.shape[1]
    group = heads // kv_heads
    total = tok * lax.axis_size("seq")
    index = lax.axis_index("seq")
    scale = width ** (-0.5)
    valid = (index > 0).astype(jnp.float32)
    edges = jnp.concatenate([keys[tok - WIN :], values[tok - WIN :]], axis=1)
    before = passed_along(edges, "seq", 1)
    ext_keys = jnp.concatenate([before[:, :kv_heads], keys], axis=0)
    ext_vals = jnp.concatenate([before[:, kv_heads:], values], axis=0).astype(jnp.float32)
    key_rows = jnp.repeat(ext_keys, group, axis=1)
    val_rows = jnp.repeat(ext_vals, group, axis=1)
    q_feat = feature_maps(
        jnp.einsum("thd,hdf->htf", queries, q_map, preferred_element_type=jnp.float32)
    )
    k_feat = feature_maps(
        jnp.einsum("thd,hdf->htf", key_rows, k_map, preferred_element_type=jnp.float32)
    )
    own_state = jnp.einsum(
        "hjf,jhd->hfd",
        k_feat[:, WIN:],
        val_rows[WIN:],
        precision=lax.Precision.HIGHEST,
        preferred_element_type=jnp.float32,
    )
    own_norm = jnp.sum(k_feat[:, WIN:], axis=1)
    edge_state = valid * jnp.einsum(
        "hjf,jhd->hfd",
        k_feat[:, :WIN],
        val_rows[:WIN],
        precision=lax.Precision.HIGHEST,
        preferred_element_type=jnp.float32,
    )
    edge_norm = valid * jnp.sum(k_feat[:, :WIN], axis=1)
    empty = (jnp.zeros_like(own_state), jnp.zeros_like(own_norm))
    prior_state, prior_norm = entering((own_state, own_norm), "seq", add_pair, empty, False)
    prior_state = prior_state - edge_state
    prior_norm = prior_norm - edge_norm
    q_pos = index * tok + jnp.arange(tok, dtype=jnp.int32)
    k_pos = index * tok - WIN + jnp.arange(tok + WIN, dtype=jnp.int32)
    near_mask = (
        (k_pos[None, :] > q_pos[:, None] - WIN)
        & (k_pos[None, :] <= q_pos[:, None])
        & (k_pos[None, :] >= 0)
    )
    far_mask = ((k_pos[None, :] <= q_pos[:, None] - WIN) & (k_pos[None, :] >= 0)).astype(
        jnp.float32
    )

    def head_pass(head):
        kv_index = head // group
        q_head = lax.dynamic_index_in_dim(queries, head, 1, keepdims=False)
        k_head = lax.dynamic_index_in_dim(ext_keys, kv_index, 1, keepdims=False)
        v_head = lax.dynamic_index_in_dim(ext_vals, kv_index, 1, keepdims=False)
        target = lax.dynamic_index_in_dim(teacher, head, 1, keepdims=False).astype(jnp.float32)
        q_head_feat = lax.dynamic_index_in_dim(q_feat, head, 0, keepdims=False)
        k_head_feat = lax.dynamic_index_in_dim(k_feat, head, 0, keepdims=False)
        state = lax.dynamic_index_in_dim(prior_state, head, 0, keepdims=False)
        norm = lax.dynamic_index_in_dim(prior_norm, head, 0, keepdims=False)
        scores = jnp.dot(q_head, k_head.T, preferred_element_type=jnp.float32) * scale
        scores = jnp.where(near_mask, scores, -1e30)
        top = jnp.max(scores, axis=-1, keepdims=True)
        weights = jnp.where(near_mask, jnp.exp(scores - top), 0.0)
        far = hdot(q_head_feat, k_head_feat.T) * far_mask
        numer = hdot(weights + far, v_head) + hdot(q_head_feat, state)
        denom = jnp.sum(weights + far, axis=-1) + hdot(q_head_feat, norm)
        out = numer / denom[:, None]
        error = out - target
        grad_out = 2.0 * error / total
        grad_num = grad_out / denom[:, None]
        grad_den = -jnp.sum(grad_out * out, axis=-1) / denom
        grad_far = (hdot(grad_num, v_head.T) + grad_den[:, None]) * far_mask
        grad_qf = (
            hdot(grad_far, k_head_feat)
            + hdot(grad_num, state.T)
            + grad_den[:, None] * norm[None, :]
        )
        grad_kf = hdot(grad_far.T, q_head_feat)
        later = hdot(q_head_feat.T, grad_num)
        later_norm = hdot(grad_den, q_head_feat)
        edge_fix = valid * (hdot(v_head[:WIN], later.T) + later_norm[None, :])
        grad_kf = grad_kf - jnp.concatenate(
            [edge_fix, jnp.zeros((tok, edge_fix.shape[1]), jnp.float32)], axis=0
        )
        return (
            out.astype(jnp.bfloat16),
            jnp.sum(error * error),
            grad_qf,
            grad_kf,
            later,
            later_norm,
        )

    outs, squares, grad_q_feat, grad_k_feat, later, later_norm = lax.map(
        head_pass, jnp.arange(heads, dtype=jnp.int32)
    )
    zero_suffix = (jnp.zeros_like(later), jnp.zeros_like(later_norm))
    suffix_state, suffix_norm = entering((later, later_norm), "seq", add_pair, zero_suffix, True)
    own_grad = jnp.einsum(
        "jhd,hfd->hjf",
        val_rows[WIN:],
        suffix_state,
        precision=lax.Precision.HIGHEST,
        preferred_element_type=jnp.float32,
    )
    own_grad = own_grad + suffix_norm[:, None, :]
    grad_k_feat = grad_k_feat + jnp.concatenate(
        [jnp.zeros((heads, WIN, own_grad.shape[2]), jnp.float32), own_grad], axis=1
    )
    grad_q_scores = map_backward(q_feat, grad_q_feat)
    grad_k_scores = map_backward(k_feat, grad_k_feat)
    grad_q_map = jnp.einsum(
        "thd,htf->hdf",
        queries.astype(jnp.float32),
        grad_q_scores,
        precision=lax.Precision.HIGHEST,
        preferred_element_type=jnp.float32,
    )
    grad_k_map = jnp.einsum(
        "jhd,hjf->hdf",
        key_rows.astype(jnp.float32),
        grad_k_scores,
        precision=lax.Precision.HIGHEST,
        preferred_element_type=jnp.float32,
    )
    grad_q_map, grad_k_map = lax.psum((grad_q_map, grad_k_map), "seq")
    loss = lax.psum(jnp.sum(squares), ("seq", "kvh")) / total
    return (jnp.swapaxes(outs, 0, 1), grad_q_map, grad_k_map, loss)


def solution(mesh):
    in_specs = (
        P("seq", "kvh", None),
        P("seq", "kvh", None),
        P("seq", "kvh", None),
        P("seq", "kvh", None),
        P("kvh", None, None),
        P("kvh", None, None),
    )
    out_specs = (P("seq", "kvh", None), P("kvh", None, None), P("kvh", None, None), P())
    return jax.shard_map(body, mesh=mesh, in_specs=in_specs, out_specs=out_specs, check_vma=False)
```

profile of v0, /device:TPU:6, one launch (start us, length us, event | category | flops | bytes accessed | tf_op | source)
XLA Modules:
  0.0 806.9 jit_solution(3412562833120047907)
XLA Ops:
  8.7 3.8 collective-permute-start
  21.6 3.0 fusion.81
  29.5 2.8 fusion.113
  32.3 2.8 fusion.112
  41.5 3.3 copy.45
  45.8 50.6 %all-gather.1 = f32[256,128]{1,0:T(8,128)} all-gather(f32[8,128]{1,0:T(8,128)S(1)} %fusion.94), channel_id=3, replica_groups=mesh['seq'=32,'kvh'=8] {'seq'}, dimensions={0}, use_global_device_ids=true | all-gather | bytes 135168 | tf_op jit(solution)/shard_map/all_gather | solution.py:17
  96.4 73.4 %all-gather.7.cloned.1.call-done = f32[256,128,128]{2,1,0:T(8,128)} async-done(((f32[8,128,128]{2,1,0:T(8,128)}), f32[256,128,128]{2,1,0:T(8,128)}) %all-gather.7.cloned.1.call-update) | async-done | bytes 16777232 | tf_op jit(solution)/shard_map/all_gather | solution.py:17
  169.8 61.8 %while.58 = (s32[]{:T(128)}, f32[8,128,128]{2,1,0:T(8,128)S(1)}, f32[8,128]{1,0:T(8,128)S(1)}, s32[]{:T(128)}, f32[32,8,128,128]{3,2,1,0:T(8,128)}, /*index=5*/f32[32,8,128]{2,1,0:T(8,128)}, s32[]{:T(128)}, s32[]{:T(128)}) while((s32[]{:T(128)}, f32[8,128,128]{2,1,0:T(8,128)S(1)}, f32[8,128]{1,0:T(8,128)S(1)}, s32[]{:T(128)}, ...), condition=%wide.region_10.11_spmd.clone, body=%wide.region_9.0_spmd.clone.sunk | while | flops 396292 | bytes 1585275 | solution.py:30
  233.0 233.5 %while.60 = (s32[]{:T(128)}, bf16[8,512,128]{1,2,0:T(8,128)(2,1)}, f32[8]{0:T(128)S(1)}, f32[8,512,128]{1,2,0:T(8,128)}, f32[8,576,128]{2,1,0:T(8,128)}, /*index...) while((s32[]{:T(128)}, bf16[8,512,128]{1,2,0:T(8,128)(2,1)}, ...), condition=%wide.region_17.18_spmd.clone.clone, body=%wide.region_12.17_spmd.clone.clone.sunk | while | flops 2664783872 | bytes 29314132 | solution.py:153
  253.9 3.2 fusion.184
  283.0 3.2 fusion.184
  312.2 3.2 fusion.184
  341.4 3.2 fusion.184
  370.6 3.2 fusion.184
  399.8 3.2 fusion.184
  429.0 3.2 fusion.184
  458.1 3.2 fusion.184
  463.0 2.8 fusion.189
  466.6 3.3 copy.52
  469.9 41.6 %all-gather.3 = f32[256,128]{1,0:T(8,128)S(1)} all-gather(f32[8,128]{1,0:T(8,128)S(1)} %get-tuple-element.513), channel_id=5, replica_groups=mesh['seq'=32,'kvh'=8] {'seq'}, dimensions={0}, use_global_device_ids=true | all-gather | bytes 135168 | tf_op jit(solution)/shard_map/all_gather | solution.py:17
  516.3 87.9 %all-gather.9.cloned.1.call-done = f32[256,128,128]{2,1,0:T(8,128)} async-done(((f32[8,128,128]{2,1,0:T(8,128)}), f32[256,128,128]{2,1,0:T(8,128)}) %all-gather.9.cloned.1.call-update) | async-done | bytes 16777232 | tf_op jit(solution)/shard_map/all_gather | solution.py:17
  604.2 40.9 %while.59 = (s32[]{:T(128)}, f32[8,128,128]{2,1,0:T(8,128)S(1)}, f32[8,128]{1,0:T(8,128)S(1)}, s32[]{:T(128)}, f32[32,8,128,128]{3,2,1,0:T(8,128)}, /*index=5*/f...) while((s32[]{:T(128)}, f32[8,128,128]{2,1,0:T(8,128)S(1)}, ...), condition=%wide.region_22.23_spmd.clone, body=%wide.region_21.22_spmd.clone.sunk | while | flops 396296 | bytes 1585337 | solution.py:30
  651.7 74.1 %psum.23 = f32[]{:T(128)} all-reduce(f32[]{:T(128)} %reduce_sum.145), channel_id=1, replica_groups=mesh['seq'=32,'kvh'=8] {'seq','kvh'}, use_global_device_ids=true, to_apply=%region_27.28 | all-reduce | flops 1 | bytes 8 | tf_op jit(solution)/shard_map/psum | solution.py:186
  727.9 67.9 %all-reduce.5.cloned.1.call-done = (f32[8,128,64]{1,2,0:T(8,128)}, f32[8,128,64]{1,2,0:T(8,128)}) async-done(((f32[8,128,64]{1,2,0:T(8,128)}, f32[8,128,64]{1,2,0:T(8,128)}), (f32[8,128,64]{1,2,0:T(8,128)}, f32[8,128,64]{1,2,0:T(8,128)})) %all-reduce.5.cloned.1.call-update) | async-done | bytes 524304 | tf_op jit(solution)/shard_map/psum | solution.py:185
  (459 shorter events, 329.8 us)
Async XLA Ops:
  7.2 8.5 %copy-start = (bf16[8,128,64]{1,2,0:T(8,128)(2,1)S(1)}, bf16[8,128,64]{1,2,0:T(8,128)(2,1)}, u32[]{:S(2)}) copy-start(bf16[8,128,64]{1,2,0:T(8,128)(2,1)} %param.17) | copy-start | bytes 393220
  7.2 162.6 %all-gather.7.cloned.1.call-start = ((), (), s32[]{:S(2)}) async-start(), calls=%async_computation | async-start | bytes 17301504 | tf_op jit(solution)/shard_map/all_gather | solution.py:17
  8.7 5.4 collective-permute-start
  15.7 3.3 copy-start.19
  21.5 210.1 %copy-start.2 = (f32[8,576,64]{1,2,0:T(8,128)}, f32[8,576,64]{1,2,0:T(8,128)S(1)}, u32[]{:S(2)}) copy-start(f32[8,576,64]{1,2,0:T(8,128)S(1)} %get-tuple-element.829) | copy-start | bytes 3538948
  24.5 579.7 %all-gather.9.cloned.1.call-start = ((), (), s32[]{:S(2)}) async-start(), calls=%async_computation.1 | async-start | bytes 17301504 | tf_op jit(solution)/shard_map/all_gather | solution.py:17
  258.6 3.6 copy-start.10
  287.8 3.6 copy-start.10
  291.4 2.6 copy-start.9
  316.9 3.6 copy-start.10
  320.6 2.6 copy-start.9
  346.1 3.6 copy-start.10
  375.3 3.7 copy-start.10
  404.5 3.6 copy-start.10
  433.7 3.6 copy-start.10
  462.9 3.6 copy-start.10
  466.5 329.3 %all-reduce.5.cloned.1.call-start = ((), (), s32[]{:S(2)}) async-start(), calls=%async_computation.2 | async-start | bytes 1048576 | tf_op jit(solution)/shard_map/psum | solution.py:185
  466.6 44.9 %copy-start.6 = (f32[8,512,64]{1,2,0:T(8,128)S(1)}, f32[8,512,64]{1,2,0:T(8,128)}, u32[]{:S(2)}) copy-start(f32[8,512,64]{1,2,0:T(8,128)} %copy-done.5) | copy-start | bytes 3145732
  511.5 2.6 copy-start.8
  511.5 2.9 copy-start.14
  511.5 3.1 copy-start.15
  604.2 40.9 %copy-start.17 = (f32[512,1,128]{2,1,0:T(1,128)S(1)}, f32[512,1,128]{2,1,0:T(1,128)}, u32[]{:S(2)}) copy-start(f32[512,1,128]{2,1,0:T(1,128)} %copy-done.16) | copy-start | bytes 786436
  649.2 76.6 %copy-start.18 = (bf16[8,512,128]{1,2,0:T(8,128)(2,1)S(1)}, bf16[8,512,128]{1,2,0:T(8,128)(2,1)}, u32[]{:S(2)}) copy-start(bf16[8,512,128]{1,2,0:T(8,128)(2,1)} %get-tuple-element.509) | copy-start | bytes 3145732
  725.8 73.4 %copy-start.1 = (bf16[8,128,64]{1,2,0:T(8,128)(2,1)S(1)}, bf16[8,128,64]{1,2,0:T(8,128)(2,1)}, u32[]{:S(2)}) copy-start(bf16[8,128,64]{1,2,0:T(8,128)(2,1)} %param.17) | copy-start | bytes 393220
  (36 other events, 67.1 us)
Sparse Core Ops, SparseCore 0:
  24.7 145.0 all-gather.6
  466.7 137.5 all-gather.8
  651.2 144.5 all-reduce.4
where the time goes:
time: 814 us; the launch traced here: 807 us
  waiting for transfers between devices  230 us (28%)
  matrix products  191 us (23%)
  blocking collectives  166 us (20%)
  other arithmetic  129 us (16%)
  local copies, waits for them, and re-layouts  53.5 us (7%)
  loops' own time  18.3 us (2%)
  between operations  15.9 us (2%)
    all_gather x2, waiting for transfers between devices, entering(): everything = jax.tree.map(lambda part: lax.all_gather(part, axis), value)  161 us
    dot_general x88, matrix products, hdot(): jnp.dot(left, right, precision=lax.Precision.HIGHEST, preferred_element_t...  160 us
    select_n x128, other arithmetic, hop(): return jax.tree.map(lambda a, b: jnp.where(reached, a, b), new, before)  101 us
    all_gather x2, blocking collectives, entering(): everything = jax.tree.map(lambda part: lax.all_gather(part, axis), value)  92.2 us
    psum x1, blocking collectives, body(): loss = lax.psum(jnp.sum(squares), ('seq', 'kvh')) / total  74.1 us
    psum x1, waiting for transfers between devices, body(): grad_q_map, grad_k_map = lax.psum((grad_q_map, grad_k_map), 'seq')  67.9 us
    another operation x1, loops' own time, body(): lax.map(head_pass, jnp.arange(heads, dtype=jnp.int32))  16.3 us
  transfers between devices with their start and end apart: 4, of which 4 were waited for; matrix products, arithmetic and copies ran while one was open for 4% of the time, Pallas kernels for 0%

commit v1 on v0

v1 whole, which is shorter than its diff:
```python
import functools

import jax
import jax.numpy as jnp
from jax import lax
from jax.experimental import pallas as pl
from jax.experimental.pallas import tpu as pltpu
from jax.sharding import PartitionSpec as P

WIN = 64
BLK = 128
F32, BF16 = jnp.float32, jnp.bfloat16
MESH = pl.DeviceIdType.MESH


def split(x):
    hi = x.astype(BF16)
    return hi, (x - hi.astype(F32)).astype(BF16)


def nn(a, b):
    return lax.dot_general(a, b, (((1,), (0,)), ((), ())), preferred_element_type=F32)


def nt(a, b):
    return lax.dot_general(a, b, (((1,), (1,)), ((), ())), preferred_element_type=F32)


def lanes(*parts):
    return jnp.concatenate(parts, axis=1)


def rows(*parts):
    return jnp.concatenate(parts, axis=0)


def peers(n, fn):
    def go(i, carry):
        fn(i)
        return carry

    lax.fori_loop(1, n, go, 0)


def remote(src, dst, send, recv, dev, axis="seq"):
    return pltpu.make_async_remote_copy(
        src_ref=src, dst_ref=dst, send_sem=send, recv_sem=recv, device_id={axis: dev}, device_id_type=MESH
    )


class Scan:
    def __init__(self, n, me, own, own_norm, got, part, out, got_norm, part_norm, out_norm, sems, norm_sems, reverse):
        self.__dict__.update(locals())
        self.chunk = own.shape[0] // n
        self.keeper = n // 2

    def piece(self, dev):
        return pl.ds(pl.multiple_of(dev * self.chunk, 8), self.chunk)

    def first(self, dev, src):
        return remote(self.own.at[self.piece(dev)], self.got.at[src], self.sems.at[0, dev], self.sems.at[1, src], dev)

    def second(self, dev, src):
        return remote(self.part.at[dev], self.out.at[self.piece(src)], self.sems.at[2, dev], self.sems.at[3, src], dev)

    def norm_first(self, src):
        return remote(self.own_norm, self.got_norm.at[src], self.norm_sems.at[0, 0], self.norm_sems.at[1, src], self.keeper)

    def norm_second(self, dev):
        return remote(self.part_norm.at[dev], self.out_norm, self.norm_sems.at[2, dev], self.norm_sems.at[0, 1], dev)

    def start(self):
        n, me = self.n, self.me

        @pl.when(me != self.keeper)
        def _():
            self.norm_first(me).start()

        peers(n, lambda i: self.first(lax.rem(me + i, n), me).start())

    def sums(self, got, part, zero):
        n = self.n

        def go(i, total):
            at = n - 1 - i if self.reverse else i
            part[at] = total
            return total + got[at]

        lax.fori_loop(0, n, go, zero)

    def turn(self):
        n, me, keeper = self.n, self.me, self.keeper
        self.got[me] = self.own[self.piece(me)]
        peers(n, lambda i: self.first(me, lax.rem(me + i, n)).wait_recv())
        self.sums(self.got, self.part, jnp.zeros((self.chunk, 128), F32))
        peers(n, lambda i: self.second(lax.rem(me + i, n), me).start())
        self.out[self.piece(me)] = self.part[me]

        @pl.when(me == keeper)
        def _():
            self.got_norm[keeper] = self.own_norm[...]
            peers(n, lambda i: self.norm_first(lax.rem(keeper + i, n)).wait_recv())
            self.sums(self.got_norm, self.part_norm, jnp.zeros((8, 128), F32))
            peers(n, lambda i: self.norm_second(lax.rem(keeper + i, n)).start())
            self.out_norm[...] = self.part_norm[keeper]

    def finish(self):
        n, me = self.n, self.me
        peers(n, lambda i: self.second(me, lax.rem(me + i, n)).wait_recv())

        @pl.when(me != self.keeper)
        def _():
            self.norm_second(me).wait_recv()

    def drain(self):
        n, me, keeper = self.n, self.me, self.keeper

        def one(i):
            dev = lax.rem(me + i, n)
            self.first(dev, me).wait_send()
            self.second(dev, me).wait_send()

        peers(n, one)

        @pl.when(me != keeper)
        def _():
            self.norm_first(me).wait_send()

        @pl.when(me == keeper)
        def _():
            peers(n, lambda i: self.norm_second(lax.rem(keeper + i, n)).wait_send())


class Total:
    def __init__(self, n, me, own, got, part, out, sems):
        self.__dict__.update(locals())
        self.chunk = own.shape[0] // n

    def piece(self, dev):
        return pl.ds(pl.multiple_of(dev * self.chunk, 8), self.chunk)

    def first(self, dev, src):
        return remote(self.own.at[self.piece(dev)], self.got.at[src], self.sems.at[0, dev], self.sems.at[1, src], dev)

    def second(self, dev, src):
        return remote(self.part, self.out.at[self.piece(src)], self.sems.at[2, dev], self.sems.at[3, src], dev)

    def start(self):
        peers(self.n, lambda i: self.first(lax.rem(self.me + i, self.n), self.me).start())

    def turn(self):
        n, me = self.n, self.me
        self.got[me] = self.own[self.piece(me)]
        peers(n, lambda i: self.first(me, lax.rem(me + i, n)).wait_recv())
        self.part[...] = lax.fori_loop(0, n, lambda i, t: t + self.got[i], jnp.zeros((self.chunk, 128), F32))
        peers(n, lambda i: self.second(lax.rem(me + i, n), me).start())
        self.out[self.piece(me)] = self.part[...]

    def finish(self):
        n, me = self.n, self.me
        peers(n, lambda i: self.second(me, lax.rem(me + i, n)).wait_recv())

    def drain(self):
        n, me = self.n, self.me

        def one(i):
            dev = lax.rem(me + i, n)
            self.first(dev, me).wait_send()
            self.second(dev, me).wait_send()

        peers(n, one)


def kernel(n, m, heads, tok, scale, inv_total, q_ref, k_ref, v_ref, t_ref, wq_ref, wk_ref,
           y_ref, gq_ref, gk_ref, loss_ref,
           tmp, kext, vext, vaug, vaugt, kt, qh, pqh, pql, pkh, pkl,
           s_own, s_norm, s_got, s_part, s_in, sn_got, sn_part, sn_in,
           loc, loc_norm, numer, gn_s, gd_s, dblk, dblk_norm,
           d_own, d_norm, d_got, d_part, d_in, dn_got, dn_part, dn_in,
           gkf, aq, aq_got, aq_part, aq_out, ak, ak_got, ak_part, ak_out,
           loss_own, loss_kv, loss_row, loss_seq,
           f_sems, fn_sems, b_sems, bn_sems, q_sems, k_sems, e_sems, lk_sems, ls_sems):
    me = lax.axis_index("seq")
    col = lax.axis_index("kvh")
    nblk = tok // BLK
    half = heads // 2

    barrier = pltpu.get_barrier_semaphore()
    peers(n, lambda i: pl.semaphore_signal(barrier, inc=1, device_id={"seq": lax.rem(me + i, n)}, device_id_type=MESH))
    peers(m, lambda i: pl.semaphore_signal(barrier, inc=1, device_id={"kvh": lax.rem(col + i, m)}, device_id_type=MESH))

    lane = lax.broadcasted_iota(jnp.int32, (1, 128), 1)
    upper = lane < 64
    ri = lax.broadcasted_iota(jnp.int32, (256, 128), 0)
    ci = lax.broadcasted_iota(jnp.int32, (256, 128), 1)
    ones2 = jnp.where((lax.rem(ri, 128) < 64) == (ci < 64), 1.0, 0.0).astype(BF16)

    def half_sums(x):
        hi, lo = split(x)
        return nn(lanes(hi, lo), ones2)

    def maps(x, w):
        w = w.astype(F32)
        a = nn(x, lanes(w, -w).astype(BF16))
        low = jnp.full_like(a, -jnp.inf)
        top = jnp.where(
            upper,
            jnp.max(jnp.where(upper, a, low), axis=-1, keepdims=True),
            jnp.max(jnp.where(upper, low, a), axis=-1, keepdims=True),
        )
        e = jnp.exp(a - top)
        return e / half_sums(e)

    def back(phi, g):
        return phi * (g - half_sums(phi * g))

    kext[WIN : WIN + tok] = k_ref[...]
    vext[WIN : WIN + tok] = v_ref[...]
    vt = v_ref[...].astype(F32).T.astype(BF16)
    vt2 = lanes(vt, vt)

    def own_keys(h, carry):
        phi = maps(k_ref[...], wk_ref[h])
        hi, lo = split(phi)
        pkh[h, WIN : WIN + tok] = hi
        pkl[h, WIN : WIN + tok] = lo
        s_own[pl.ds(pl.multiple_of(h * 128, 128), 128)] = nn(vt2, rows(hi, lo))
        s_norm[pl.ds(h, 1)] = jnp.sum(phi, axis=0, keepdims=True)
        return carry

    lax.fori_loop(0, heads, own_keys, 0)
    pl.semaphore_wait(barrier, n - 1 + m - 1)

    def edge_copy(i, dev):
        src, dst = (k_ref, kext) if i == 0 else (v_ref, vext)
        return remote(src.at[pl.ds(tok - WIN, WIN)], dst.at[pl.ds(0, WIN)], e_sems.at[0, i], e_sems.at[1, i], dev)

    @pl.when(me < n - 1)
    def _():
        edge_copy(0, me + 1).start()
        edge_copy(1, me + 1).start()

    fwd = Scan(n, me, s_own, s_norm, s_got, s_part, s_in, sn_got, sn_part, sn_in, f_sems, fn_sems, False)
    bwd = Scan(n, me, d_own, d_norm, d_got, d_part, d_in, dn_got, dn_part, dn_in, b_sems, bn_sems, True)
    fwd.start()

    tmp[...] = q_ref[...].astype(F32)

    def query_maps(h, carry):
        x = tmp[pl.ds(h, tok, stride=heads), :].astype(BF16)
        qh[h] = x
        hi, lo = split(maps(x, wq_ref[h]))
        pqh[h] = hi
        pql[h] = lo
        return carry

    lax.fori_loop(0, heads, query_maps, 0)

    @pl.when(me == 0)
    def _():
        kext[0:WIN] = jnp.zeros((WIN, 128), BF16)
        vext[0:WIN] = jnp.zeros((WIN, 128), BF16)

    @pl.when(me > 0)
    def _():
        edge_copy(0, me - 1).wait_recv()
        edge_copy(1, me - 1).wait_recv()

    pad = jnp.zeros((WIN, 128), BF16)
    kext[WIN + tok :] = pad
    vext[WIN + tok :] = pad
    valid = jnp.where(me > 0, 1.0, 0.0).astype(F32)
    vaug[:, 0:128] = vext[...]
    vaug[:, 128:256] = jnp.ones((tok + 2 * WIN, 128), BF16)
    vaugt[0:128] = vext[0:tok].astype(F32).T.astype(BF16)
    vaugt[128:256] = jnp.ones((128, tok), BF16)
    kt[...] = kext[0:tok].astype(F32).T.astype(BF16)

    def edge_maps(h, carry):
        phi = maps(kext[0:WIN], wk_ref[h]) * valid
        hi, lo = split(phi)
        pkh[h, 0:WIN] = hi
        pkl[h, 0:WIN] = lo
        return carry

    lax.fori_loop(0, heads, edge_maps, 0)
    fwd.turn()

    r2 = lax.broadcasted_iota(jnp.int32, (BLK, 2 * BLK), 0)
    c2 = lax.broadcasted_iota(jnp.int32, (BLK, 2 * BLK), 1)
    near_band = (c2 > r2) & (c2 <= r2 + WIN)
    first_key = jnp.where(me > 0, 0, WIN)
    r1 = lax.broadcasted_iota(jnp.int32, (BLK, BLK), 0)
    c1 = lax.broadcasted_iota(jnp.int32, (BLK, BLK), 1)
    causal = c1 <= r1

    def local_forward(h, carry):
        ph0 = pkh[h, 0:WIN]
        pl0 = pkl[h, 0:WIN]
        zero = jnp.zeros((WIN, 128), BF16)
        vb = vaugt[:, 0:BLK]
        state = -nn(lanes(vb, vb), rows(ph0, zero, pl0, zero))
        for b in range(nblk):
            at = b * BLK
            loc[h, b] = state[0:128]
            loc_norm[h, b] = state[128:136]
            kh = pkh[h, at : at + BLK]
            kl = pkl[h, at : at + BLK]
            qhi = pqh[h, at : at + BLK]
            qlo = pql[h, at : at + BLK]
            q3 = lanes(qhi, qlo, qhi)
            far = jnp.where(causal, nt(q3, lanes(kh, kh, kl)), 0.0)
            s = nt(qh[h, at : at + BLK], kext[at : at + 2 * BLK]) * scale
            mask = near_band & (c2 >= first_key) if b == 0 else near_band
            s = jnp.where(mask, s, -1e30)
            top = jnp.max(s, axis=-1, keepdims=True)
            w = jnp.where(mask, jnp.exp(s - top), 0.0)
            w = lanes(w[:, 0:BLK] + far, w[:, BLK:])
            whi, wlo = split(w)
            va = vaug[at : at + 2 * BLK]
            shi, slo = split(state)
            numer[h, at : at + BLK] = nn(lanes(whi, wlo), rows(va, va)) + nt(q3, lanes(shi, shi, slo))
            if b + 1 < nblk:
                vb = vaugt[:, at : at + BLK]
                state = state + nn(lanes(vb, vb), rows(kh, kl))
        return carry

    lax.fori_loop(0, heads, local_forward, 0)
    fwd.finish()

    tmp[...] = t_ref[...].astype(F32)

    def outputs(h, squares):
        prior = s_in[pl.ds(pl.multiple_of(h * 128, 128), 128)]
        prior_norm = jnp.broadcast_to(sn_in[pl.ds(h, 1)], (128, 128))
        shi, slo = split(rows(prior, prior_norm))
        s3 = lanes(shi, shi, slo)
        d_sum = jnp.zeros((128, 128), F32)
        dn_sum = jnp.zeros((1, 128), F32)
        for b in range(nblk):
            at = b * BLK
            qhi = pqh[h, at : at + BLK]
            qlo = pql[h, at : at + BLK]
            both = numer[h, at : at + BLK] + nt(lanes(qhi, qlo, qhi), s3)
            den = both[:, 128:256]
            y = both[:, 0:128] / den
            where = pl.ds(h + at * heads, BLK, stride=heads)
            error = y - tmp[where, :]
            tmp[where, :] = y
            squares = squares + jnp.sum((error * error).reshape(BLK // 8, 8, 128), axis=0)
            gn = (2.0 * inv_total) * error / den
            gd = jnp.broadcast_to(-jnp.sum(gn * y, axis=-1, keepdims=True), (BLK, 128))
            gn_s[h, at : at + BLK] = gn
            gd_s[h, at : at + BLK] = gd
            ghi, glo = split(gn.T)
            d = nn(lanes(ghi, glo, ghi), rows(qhi, qhi, qlo))
            dn = jnp.sum(gd * (qhi.astype(F32) + qlo.astype(F32)), axis=0, keepdims=True)
            dblk[h, b] = d
            dblk_norm[h, b] = jnp.broadcast_to(dn, (8, 128))
            d_sum = d_sum + d
            dn_sum = dn_sum + dn
        d_own[pl.ds(pl.multiple_of(h * 128, 128), 128)] = d_sum
        d_norm[pl.ds(h, 1)] = dn_sum
        return squares

    loss_own[...] = lax.fori_loop(0, heads, outputs, jnp.zeros((8, 128), F32))
    bwd.start()

    def loss_cols(dev, src):
        return remote(loss_own, loss_kv.at[src], lk_sems.at[0, dev], lk_sems.at[1, src], dev, "kvh")

    def loss_rows(dev, src):
        return remote(loss_row, loss_seq.at[src], ls_sems.at[0, dev], ls_sems.at[1, src], dev)

    peers(m, lambda i: loss_cols(lax.rem(col + i, m), col).start())
    y_ref[...] = tmp[...].astype(BF16)

    def local_backward(h, carry):
        prior = s_in[pl.ds(pl.multiple_of(h * 128, 128), 128)]
        prior_norm = sn_in[pl.ds(h, 1)]
        later = jnp.zeros((128, 128), F32)
        later_norm = jnp.zeros((1, 128), F32)
        g = jnp.zeros((128, 128), F32)
        for b in reversed(range(nblk)):
            at = b * BLK
            gn = gn_s[h, at : at + BLK]
            gd = gd_s[h, at : at + BLK]
            vb = vext[at : at + BLK]
            kh = pkh[h, at : at + BLK]
            kl = pkl[h, at : at + BLK]
            qhi = pqh[h, at : at + BLK]
            qlo = pql[h, at : at + BLK]
            ghi, glo = split(gn)
            gf = jnp.where(causal, nt(lanes(ghi, glo), lanes(vb, vb)) + gd, 0.0)
            fhi, flo = split(gf)
            shi, slo = split(prior + loc[h, b])
            norm = prior_norm + loc_norm[h, b, 0:1]
            gqf = nn(lanes(fhi, flo, fhi, ghi, glo, ghi), rows(kh, kh, kl, shi, shi, slo)) + gd * norm
            rhi, rlo = split(back(qhi.astype(F32) + qlo.astype(F32), gqf))
            qt = qh[h, at : at + BLK].astype(F32).T.astype(BF16)
            g = g + nn(lanes(qt, qt), rows(rhi, rlo))
            thi, tlo = split(gf.T)
            lhi, llo = split(later)
            gkf[h, at : at + BLK] = (
                nn(lanes(thi, tlo, thi, vb, vb), rows(qhi, qhi, qlo, lhi, llo)) + later_norm
            )
            later = later + dblk[h, b]
            later_norm = later_norm + dblk_norm[h, b, 0:1]
        put(aq, h, g)
        return carry

    def put(ref, h, g):
        g = g - pltpu.roll(g, 64, 1)

        @pl.when(h < half)
        def _():
            ref[pl.ds(pl.multiple_of(h * 128, 128), 128)] = jnp.where(upper, g, 0.0)

        @pl.when(h >= half)
        def _():
            at = pl.ds(pl.multiple_of((h - half) * 128, 128), 128)
            ref[at] = jnp.where(upper, ref[at], -g)

    split_at = heads // 2
    lax.fori_loop(0, split_at, local_backward, 0)
    bwd.turn()
    lax.fori_loop(split_at, heads, local_backward, 0)
    q_total = Total(n, me, aq, aq_got, aq_part, aq_out, q_sems)
    k_total = Total(n, me, ak, ak_got, ak_part, ak_out, k_sems)
    q_total.start()
    loss_kv[col] = loss_own[...]
    peers(m, lambda i: loss_cols(col, lax.rem(col + i, m)).wait_recv())
    loss_row[...] = lax.fori_loop(0, m, lambda i, t: t + loss_kv[i], jnp.zeros((8, 128), F32))
    peers(n, lambda i: loss_rows(lax.rem(me + i, n), me).start())
    bwd.finish()

    def key_grads(h, carry):
        shi, slo = split(d_in[pl.ds(pl.multiple_of(h * 128, 128), 128)])
        suffix_norm = dn_in[pl.ds(h, 1)]
        v = vext[0:tok]
        g = gkf[h] + nn(lanes(v, v), rows(shi, slo)) + suffix_norm
        hi, lo = split(back(pkh[h, 0:tok].astype(F32) + pkl[h, 0:tok].astype(F32), g))
        t = kt[...]
        put(ak, h, nn(lanes(t, t), rows(hi, lo)))
        return carry

    lax.fori_loop(0, heads, key_grads, 0)
    k_total.start()
    q_total.turn()
    k_total.turn()

    loss_seq[me] = loss_row[...]
    peers(n, lambda i: loss_rows(me, lax.rem(me + i, n)).wait_recv())
    total = lax.fori_loop(0, n, lambda i, t: t + loss_seq[i], jnp.zeros((8, 128), F32))
    loss_ref[...] = jnp.broadcast_to(jnp.sum(total) * inv_total, (8, 128))

    def unpack(src, dst):
        for h in range(half):
            x = src[h * 128 : (h + 1) * 128]
            dst[h] = x[:, 0:64]
            dst[h + half] = pltpu.roll(x, 64, 1)[:, 0:64]

    q_total.finish()
    unpack(aq_out, gq_ref)
    k_total.finish()
    unpack(ak_out, gk_ref)

    fwd.drain()
    bwd.drain()
    q_total.drain()
    k_total.drain()

    @pl.when(me < n - 1)
    def _():
        edge_copy(0, me + 1).wait_send()
        edge_copy(1, me + 1).wait_send()

    peers(m, lambda i: loss_cols(lax.rem(col + i, m), col).wait_send())
    peers(n, lambda i: loss_rows(lax.rem(me + i, n), me).wait_send())


def body(queries, keys, values, teacher, q_map, k_map):
    tok, heads, width = queries.shape
    n, m = lax.axis_size("seq"), lax.axis_size("kvh")
    nblk = tok // BLK
    vmem = lambda shape, dtype=F32: pltpu.VMEM(shape, dtype)
    dma = lambda *shape: pltpu.SemaphoreType.DMA(shape)
    state = heads * 128
    grad = heads * 64
    scan_bufs = lambda: [
        vmem((state, 128)),
        vmem((8, 128)),
        vmem((n, state // n, 128)),
        vmem((n, state // n, 128)),
        vmem((state, 128)),
        vmem((n, 8, 128)),
        vmem((n, 8, 128)),
        vmem((8, 128)),
    ]
    total_bufs = lambda: [vmem((grad, 128)), vmem((n, grad // n, 128)), vmem((grad // n, 128)), vmem((grad, 128))]
    spec = pl.BlockSpec(memory_space=pltpu.VMEM)
    outs, grad_q, grad_k, loss = pl.pallas_call(
        functools.partial(kernel, n, m, heads, tok, width**-0.5, 1.0 / (tok * n)),
        out_shape=(
            jax.ShapeDtypeStruct((tok * heads, width), BF16),
            jax.ShapeDtypeStruct(q_map.shape, F32),
            jax.ShapeDtypeStruct(k_map.shape, F32),
            jax.ShapeDtypeStruct((8, 128), F32),
        ),
        in_specs=[spec] * 6,
        out_specs=(spec,) * 4,
        scratch_shapes=[
            vmem((tok * heads, width)),
            vmem((tok + 2 * WIN, 128), BF16),
            vmem((tok + 2 * WIN, 128), BF16),
            vmem((tok + 2 * WIN, 256), BF16),
            vmem((256, tok), BF16),
            vmem((128, tok), BF16),
            vmem((heads, tok, 128), BF16),
            vmem((heads, tok, 128), BF16),
            vmem((heads, tok, 128), BF16),
            vmem((heads, tok + WIN, 128), BF16),
            vmem((heads, tok + WIN, 128), BF16),
            *scan_bufs(),
            vmem((heads, nblk, 128, 128)),
            vmem((heads, nblk, 8, 128)),
            vmem((heads, tok, 256)),
            vmem((heads, tok, 128)),
            vmem((heads, tok, 128)),
            vmem((heads, nblk, 128, 128)),
            vmem((heads, nblk, 8, 128)),
            *scan_bufs(),
            vmem((heads, tok, 128)),
            *total_bufs(),
            *total_bufs(),
            vmem((8, 128)),
            vmem((m, 8, 128)),
            vmem((8, 128)),
            vmem((n, 8, 128)),
            dma(4, n),
            dma(3, n),
            dma(4, n),
            dma(3, n),
            dma(4, n),
            dma(4, n),
            dma(2, 2),
            dma(2, m),
            dma(2, n),
        ],
        compiler_params=pltpu.CompilerParams(collective_id=1, has_side_effects=True, vmem_limit_bytes=58 << 20),
    )(
        queries.reshape(tok * heads, width),
        keys.reshape(tok, width),
        values.reshape(tok, width),
        teacher.reshape(tok * heads, width),
        q_map,
        k_map,
    )
    return outs.reshape(tok, heads, width), grad_q, grad_k, loss[0, 0]


def solution(mesh):
    in_specs = (
        P("seq", "kvh", None),
        P("seq", "kvh", None),
        P("seq", "kvh", None),
        P("seq", "kvh", None),
        P("kvh", None, None),
        P("kvh", None, None),
    )
    out_specs = (P("seq", "kvh", None), P("kvh", None, None), P("kvh", None, None), P())
    return jax.shard_map(body, mesh=mesh, in_specs=in_specs, out_specs=out_specs, check_vma=False)
```

time: 814 us -> 127 us (0.16)
  waiting for transfers between devices: 230 us -> 0 us
  matrix products: 191 us -> 0 us
  blocking collectives: 166 us -> 0 us
  other arithmetic: 129 us -> 0 us
  Pallas kernels: 0 us -> 117 us
  local copies, waits for them, and re-layouts: 53.5 us -> 8.74 us
  loops' own time: 18.3 us -> 0 us
  between operations: 15.9 us -> 0.66 us
    dot_general x101 -> x0, matrix products: 182 us -> none  [the longest x88 160 us: hdot(): jnp.dot(left, right, precision=lax.Precision.HIGHEST, preferred_element_t...]
    all_gather x2 -> x0, waiting for transfers between devices: 161 us -> none  [entering(): everything = jax.tree.map(lambda part: lax.all_gather(part, axis), value)]
    pallas_call x0 -> x1, Pallas kernels: none -> 117 us  [body(): pl.pallas_call(functools.partial(kernel, n, m, heads, tok, width ** (-0.5...]
    select_n x128 -> x0, other arithmetic: 101 us -> none  [hop(): return jax.tree.map(lambda a, b: jnp.where(reached, a, b), new, before)]
    all_gather x2 -> x0, blocking collectives: 92.2 us -> none  [entering(): everything = jax.tree.map(lambda part: lax.all_gather(part, axis), value)]
    psum x1 -> x0, blocking collectives: 74.1 us -> none  [body(): loss = lax.psum(jnp.sum(squares), ('seq', 'kvh')) / total]
    psum x1 -> x0, waiting for transfers between devices: 67.9 us -> none  [body(): grad_q_map, grad_k_map = lax.psum((grad_q_map, grad_k_map), 'seq')]
    another operation x3 -> x0, loops' own time: 18.3 us -> none  [the longest x1 16.3 us: body(): lax.map(head_pass, jnp.arange(heads, dtype=jnp.int32))]
  transfers between devices with their start and end apart: 4 -> 0, of which waited for: 4 -> 0; matrix products, arithmetic and copies ran while one was open for 4% -> 0% of each run, Pallas kernels for 0% -> 0%
where the time goes in v1:
time: 127 us; the launch traced here: 126 us
  Pallas kernels  117 us (92%)
  local copies, waits for them, and re-layouts  8.74 us (7%)
    pallas_call x1, Pallas kernels, body(): pl.pallas_call(functools.partial(kernel, n, m, heads, tok, width ** (-0.5...  117 us
    unnamed x9, local copies, waits for them, and re-layouts  7.46 us

profile of v1, /device:TPU:6, one launch (start us, length us, event | category | flops | bytes accessed | tf_op | source)
XLA Modules:
  0.0 126.0 jit_solution(6706097380804666863)
XLA Ops:
  0.6 0.0 copy-start.1
  0.6 1.8 %copy.10.wq_ref = bf16[8,128,64]{2,1,0:T(8,128)(2,1)} copy(bf16[8,128,64]{1,2,0:T(8,128)(2,1)} %param.10) | data formatting | bytes 262144 | tf_op args[4]
  2.4 0.0 copy-done.1
  2.4 0.9 copy.11.wk_ref
  3.3 116.6 %shard_map.93 = (bf16[4096,128]{1,0:T(8,128)(2,1)}, f32[8,128,64]{2,1,0:T(8,128)}, f32[8,128,64]{2,1,0:T(8,128)}, f32[8,128]{1,0:T(8,128)}) custom-call(bf16[4096,128]{1,0:T(8,128)(2,1)} %bitcast.7, bf16[512,128]{1,0:T(8,128)(2,1)} %bitcast.9, bf16[512,128]{1,0:T(8,128)(2,1)} %bitcast.10, bf16[4096,128]{1,0:T(8,128)(2,1)} %bitcast.8, ...), custom_call_target="tpu_custom_call" | custom-call | tf_op jit(solution)/shard_map/pallas_call | solution.py:502
  119.8 0.0 copy-start
  119.8 1.3 %slice.3 = f32[1,1]{1,0:T(1,128)} slice(f32[8,128]{1,0:T(8,128)} %get-tuple-element.11), slice={[0:1], [0:1]} | slice | bytes 8 | tf_op jit(solution)/shard_map/slice | solution.py:559
  121.1 1.9 %copy.12 = f32[8,128,64]{1,2,0:T(8,128)} copy(f32[8,128,64]{2,1,0:T(8,128)} %get-tuple-element.13) | data formatting | bytes 524288
  123.1 1.9 %copy.13 = f32[8,128,64]{1,2,0:T(8,128)} copy(f32[8,128,64]{2,1,0:T(8,128)} %get-tuple-element.14) | data formatting | bytes 524288
  125.0 0.0 copy-done
  125.0 1.0 copy.15
Async XLA Ops:
  0.6 1.8 %copy-start.1 = (bf16[8,128,64]{1,2,0:T(8,128)(2,1)S(1)}, bf16[8,128,64]{1,2,0:T(8,128)(2,1)}, u32[]{:S(2)}) copy-start(bf16[8,128,64]{1,2,0:T(8,128)(2,1)} %param.11) | copy-start | bytes 393220
  119.8 5.1 %copy-start = (bf16[4096,128]{1,0:T(8,128)(2,1)S(1)}, bf16[4096,128]{1,0:T(8,128)(2,1)}, u32[]{:S(2)}) copy-start(bf16[4096,128]{1,0:T(8,128)(2,1)} %get-tuple-element.8) | copy-start | bytes 3145732

commit v2 on v1

--- a/solution.py
+++ b/solution.py
@@ -57,26 +57,40 @@
     def piece(self, dev):
         return pl.ds(pl.multiple_of(dev * self.chunk, 8), self.chunk)
 
-    def first(self, dev, src):
-        return remote(self.own.at[self.piece(dev)], self.got.at[src], self.sems.at[0, dev], self.sems.at[1, src], dev)
-
-    def second(self, dev, src):
-        return remote(self.part.at[dev], self.out.at[self.piece(src)], self.sems.at[2, dev], self.sems.at[3, src], dev)
-
-    def norm_first(self, src):
-        return remote(self.own_norm, self.got_norm.at[src], self.norm_sems.at[0, 0], self.norm_sems.at[1, src], self.keeper)
+    def next(self):
+        return lax.rem(self.me + 1, self.n)
+
+    def first(self, dev):
+        return remote(self.own.at[self.piece(dev)], self.got.at[self.me], self.sems.at[0], self.sems.at[1], dev)
+
+    def second(self, dev):
+        return remote(self.part.at[dev], self.out.at[self.piece(self.me)], self.sems.at[2], self.sems.at[3], dev)
+
+    def all_first(self):
+        block = self.got.at[pl.ds(0, self.n - 1)]
+        return remote(block, block, self.sems.at[0], self.sems.at[1], self.next())
+
+    def all_second(self):
+        block = self.out.at[pl.ds(0, (self.n - 1) * self.chunk)]
+        return remote(block, block, self.sems.at[2], self.sems.at[3], self.next())
+
+    def norm_first(self):
+        return remote(self.own_norm, self.got_norm.at[self.me], self.norm_sems.at[0], self.norm_sems.at[1], self.keeper)
 
     def norm_second(self, dev):
-        return remote(self.part_norm.at[dev], self.out_norm, self.norm_sems.at[2, dev], self.norm_sems.at[0, 1], dev)
+        return remote(self.part_norm.at[dev], self.out_norm, self.norm_sems.at[2], self.norm_sems.at[3], dev)
+
+    def all_norms(self):
+        block = self.got_norm.at[pl.ds(0, self.n - 1)]
+        return remote(block, block, self.norm_sems.at[2], self.norm_sems.at[1], self.next())
 
     def start(self):
         n, me = self.n, self.me
+        peers(n, lambda i: self.first(lax.rem(me + i, n)).start())
 
         @pl.when(me != self.keeper)
         def _():
-            self.norm_first(me).start()
-
-        peers(n, lambda i: self.first(lax.rem(me + i, n), me).start())
+            self.norm_first().start()
 
     def sums(self, got, part, zero):
         n = self.n
@@ -86,49 +100,43 @@
             part[at] = total
             return total + got[at]
 
-        lax.fori_loop(0, n, go, zero)
+        return lax.fori_loop(0, n, go, zero)
 
     def turn(self):
         n, me, keeper = self.n, self.me, self.keeper
         self.got[me] = self.own[self.piece(me)]
-        peers(n, lambda i: self.first(me, lax.rem(me + i, n)).wait_recv())
+        self.all_first().wait_recv()
         self.sums(self.got, self.part, jnp.zeros((self.chunk, 128), F32))
-        peers(n, lambda i: self.second(lax.rem(me + i, n), me).start())
+        peers(n, lambda i: self.second(lax.rem(me + i, n)).start())
         self.out[self.piece(me)] = self.part[me]
 
         @pl.when(me == keeper)
         def _():
             self.got_norm[keeper] = self.own_norm[...]
-            peers(n, lambda i: self.norm_first(lax.rem(keeper + i, n)).wait_recv())
-            self.sums(self.got_norm, self.part_norm, jnp.zeros((8, 128), F32))
+            self.all_norms().wait_recv()
+            total = self.sums(self.got_norm, self.part_norm, jnp.zeros((16, 128), F32))
+            self.part_norm[:, 8:16] = jnp.broadcast_to(total[None, 8:16], (n, 8, 128))
             peers(n, lambda i: self.norm_second(lax.rem(keeper + i, n)).start())
             self.out_norm[...] = self.part_norm[keeper]
 
     def finish(self):
-        n, me = self.n, self.me
-        peers(n, lambda i: self.second(me, lax.rem(me + i, n)).wait_recv())
-
-        @pl.when(me != self.keeper)
+        self.all_second().wait_recv()
+
+        @pl.when(self.me != self.keeper)
         def _():
-            self.norm_second(me).wait_recv()
+            self.norm_second(self.next()).wait_recv()
 
     def drain(self):
-        n, me, keeper = self.n, self.me, self.keeper
-
-        def one(i):
-            dev = lax.rem(me + i, n)
-            self.first(dev, me).wait_send()
-            self.second(dev, me).wait_send()
-
-        peers(n, one)
-
-        @pl.when(me != keeper)
+        self.all_first().wait_send()
+        self.all_second().wait_send()
+
+        @pl.when(self.me != self.keeper)
         def _():
-            self.norm_first(me).wait_send()
-
-        @pl.when(me == keeper)
+            self.norm_first().wait_send()
+
+        @pl.when(self.me == self.keeper)
         def _():
-            peers(n, lambda i: self.norm_second(lax.rem(keeper + i, n)).wait_send())
+            self.all_norms().wait_send()
 
 
 class Total:
@@ -139,55 +147,72 @@
     def piece(self, dev):
         return pl.ds(pl.multiple_of(dev * self.chunk, 8), self.chunk)
 
-    def first(self, dev, src):
-        return remote(self.own.at[self.piece(dev)], self.got.at[src], self.sems.at[0, dev], self.sems.at[1, src], dev)
-
-    def second(self, dev, src):
-        return remote(self.part, self.out.at[self.piece(src)], self.sems.at[2, dev], self.sems.at[3, src], dev)
+    def next(self):
+        return lax.rem(self.me + 1, self.n)
+
+    def first(self, dev):
+        return remote(self.own.at[self.piece(dev)], self.got.at[self.me], self.sems.at[0], self.sems.at[1], dev)
+
+    def second(self, dev):
+        return remote(self.part, self.out.at[self.piece(self.me)], self.sems.at[2], self.sems.at[3], dev)
+
+    def all_first(self):
+        block = self.got.at[pl.ds(0, self.n - 1)]
+        return remote(block, block, self.sems.at[0], self.sems.at[1], self.next())
+
+    def all_second(self):
+        block = self.out.at[pl.ds(0, (self.n - 1) * self.chunk)]
+        return remote(block, block, self.sems.at[2], self.sems.at[3], self.next())
 
     def start(self):
-        peers(self.n, lambda i: self.first(lax.rem(self.me + i, self.n), self.me).start())
+        peers(self.n, lambda i: self.first(lax.rem(self.me + i, self.n)).start())
 
     def turn(self):
         n, me = self.n, self.me
         self.got[me] = self.own[self.piece(me)]
-        peers(n, lambda i: self.first(me, lax.rem(me + i, n)).wait_recv())
+        self.all_first().wait_recv()
         self.part[...] = lax.fori_loop(0, n, lambda i, t: t + self.got[i], jnp.zeros((self.chunk, 128), F32))
-        peers(n, lambda i: self.second(lax.rem(me + i, n), me).start())
+        peers(n, lambda i: self.second(lax.rem(me + i, n)).start())
         self.out[self.piece(me)] = self.part[...]
 
     def finish(self):
-        n, me = self.n, self.me
-        peers(n, lambda i: self.second(me, lax.rem(me + i, n)).wait_recv())
+        self.all_second().wait_recv()
 
     def drain(self):
-        n, me = self.n, self.me
-
-        def one(i):
-            dev = lax.rem(me + i, n)
-            self.first(dev, me).wait_send()
-            self.second(dev, me).wait_send()
-
-        peers(n, one)
-
-
-def kernel(n, m, heads, tok, scale, inv_total, q_ref, k_ref, v_ref, t_ref, wq_ref, wk_ref,
-           y_ref, gq_ref, gk_ref, loss_ref,
+        self.all_first().wait_send()
+        self.all_second().wait_send()
+
+
+def each(lo, hi, fn, init=0, unroll=2):
+    def go(i, carry):
+        for u in range(unroll):
+            carry = fn(lo + i * unroll + u, carry)
+        return carry
+
+    return lax.fori_loop(0, (hi - lo) // unroll, go, init)
+
+
+def kernel(n, m, heads, tok, scale, inv_total, q_hbm, k_ref, v_ref, t_hbm, wq_ref, wk_ref,
+           y_hbm, gq_ref, gk_ref, loss_ref,
            tmp, kext, vext, vaug, vaugt, kt, qh, pqh, pql, pkh, pkl,
            s_own, s_norm, s_got, s_part, s_in, sn_got, sn_part, sn_in,
            loc, loc_norm, numer, gn_s, gd_s, dblk, dblk_norm,
            d_own, d_norm, d_got, d_part, d_in, dn_got, dn_part, dn_in,
            gkf, aq, aq_got, aq_part, aq_out, ak, ak_got, ak_part, ak_out,
-           loss_own, loss_kv, loss_row, loss_seq,
-           f_sems, fn_sems, b_sems, bn_sems, q_sems, k_sems, e_sems, lk_sems, ls_sems):
+           loss_row, loss_kv, q_ref, t_ref, y_ref,
+           f_sems, fn_sems, b_sems, bn_sems, q_sems, k_sems, e_sems, lk_sems, io_sems):
     me = lax.axis_index("seq")
     col = lax.axis_index("kvh")
     nblk = tok // BLK
-    half = heads // 2
 
     barrier = pltpu.get_barrier_semaphore()
     peers(n, lambda i: pl.semaphore_signal(barrier, inc=1, device_id={"seq": lax.rem(me + i, n)}, device_id_type=MESH))
     peers(m, lambda i: pl.semaphore_signal(barrier, inc=1, device_id={"kvh": lax.rem(col + i, m)}, device_id_type=MESH))
+    load_q = pltpu.make_async_copy(q_hbm, q_ref, io_sems.at[0])
+    load_t = pltpu.make_async_copy(t_hbm, t_ref, io_sems.at[1])
+    save_y = pltpu.make_async_copy(y_ref, y_hbm, io_sems.at[2])
+    load_q.start()
+    load_t.start()
 
     lane = lax.broadcasted_iota(jnp.int32, (1, 128), 1)
     upper = lane < 64
@@ -201,7 +226,7 @@
 
     def maps(x, w):
         w = w.astype(F32)
-        a = nn(x, lanes(w, -w).astype(BF16))
+        a = nt(x, rows(w, -w).astype(BF16))
         low = jnp.full_like(a, -jnp.inf)
         top = jnp.where(
             upper,
@@ -228,7 +253,8 @@
         s_norm[pl.ds(h, 1)] = jnp.sum(phi, axis=0, keepdims=True)
         return carry
 
-    lax.fori_loop(0, heads, own_keys, 0)
+    each(0, heads, own_keys)
+    s_norm[8:16] = jnp.zeros((8, 128), F32)
     pl.semaphore_wait(barrier, n - 1 + m - 1)
 
     def edge_copy(i, dev):
@@ -244,6 +270,7 @@
     bwd = Scan(n, me, d_own, d_norm, d_got, d_part, d_in, dn_got, dn_part, dn_in, b_sems, bn_sems, True)
     fwd.start()
 
+    load_q.wait()
     tmp[...] = q_ref[...].astype(F32)
 
     def query_maps(h, carry):
@@ -254,7 +281,7 @@
         pql[h] = lo
         return carry
 
-    lax.fori_loop(0, heads, query_maps, 0)
+    each(0, heads, query_maps)
 
     @pl.when(me == 0)
     def _():
@@ -283,8 +310,7 @@
         pkl[h, 0:WIN] = lo
         return carry
 
-    lax.fori_loop(0, heads, edge_maps, 0)
-    fwd.turn()
+    each(0, heads, edge_maps)
 
     r2 = lax.broadcasted_iota(jnp.int32, (BLK, 2 * BLK), 0)
     c2 = lax.broadcasted_iota(jnp.int32, (BLK, 2 * BLK), 1)
@@ -325,9 +351,12 @@
                 state = state + nn(lanes(vb, vb), rows(kh, kl))
         return carry
 
-    lax.fori_loop(0, heads, local_forward, 0)
+    each(0, heads // 2, local_forward)
+    fwd.turn()
+    each(heads // 2, heads, local_forward)
     fwd.finish()
 
+    load_t.wait()
     tmp[...] = t_ref[...].astype(F32)
 
     def outputs(h, squares):
@@ -363,17 +392,14 @@
         d_norm[pl.ds(h, 1)] = dn_sum
         return squares
 
-    loss_own[...] = lax.fori_loop(0, heads, outputs, jnp.zeros((8, 128), F32))
+    d_norm[8:16] = each(0, heads, outputs, jnp.zeros((8, 128), F32))
     bwd.start()
 
     def loss_cols(dev, src):
-        return remote(loss_own, loss_kv.at[src], lk_sems.at[0, dev], lk_sems.at[1, src], dev, "kvh")
-
-    def loss_rows(dev, src):
-        return remote(loss_row, loss_seq.at[src], ls_sems.at[0, dev], ls_sems.at[1, src], dev)
-
-    peers(m, lambda i: loss_cols(lax.rem(col + i, m), col).start())
+        return remote(loss_row, loss_kv.at[src], lk_sems.at[0, dev], lk_sems.at[1, src], dev, "kvh")
+
     y_ref[...] = tmp[...].astype(BF16)
+    save_y.start()
 
     def local_backward(h, carry):
         prior = s_in[pl.ds(pl.multiple_of(h * 128, 128), 128)]
@@ -410,29 +436,18 @@
         return carry
 
     def put(ref, h, g):
-        g = g - pltpu.roll(g, 64, 1)
-
-        @pl.when(h < half)
-        def _():
-            ref[pl.ds(pl.multiple_of(h * 128, 128), 128)] = jnp.where(upper, g, 0.0)
-
-        @pl.when(h >= half)
-        def _():
-            at = pl.ds(pl.multiple_of((h - half) * 128, 128), 128)
-            ref[at] = jnp.where(upper, ref[at], -g)
-
-    split_at = heads // 2
-    lax.fori_loop(0, split_at, local_backward, 0)
+        g = g.T
+        ref[pl.ds(pl.multiple_of(h * 64, 64), 64)] = g[0:64] - g[64:128]
+
+    each(0, heads // 2, local_backward)
     bwd.turn()
-    lax.fori_loop(split_at, heads, local_backward, 0)
+    each(heads // 2, heads, local_backward)
     q_total = Total(n, me, aq, aq_got, aq_part, aq_out, q_sems)
     k_total = Total(n, me, ak, ak_got, ak_part, ak_out, k_sems)
     q_total.start()
-    loss_kv[col] = loss_own[...]
-    peers(m, lambda i: loss_cols(col, lax.rem(col + i, m)).wait_recv())
-    loss_row[...] = lax.fori_loop(0, m, lambda i, t: t + loss_kv[i], jnp.zeros((8, 128), F32))
-    peers(n, lambda i: loss_rows(lax.rem(me + i, n), me).start())
     bwd.finish()
+    loss_row[...] = dn_in[8:16]
+    peers(m, lambda i: loss_cols(lax.rem(col + i, m), col).start())
 
     def key_grads(h, carry):
         shi, slo = split(d_in[pl.ds(pl.multiple_of(h * 128, 128), 128)])
@@ -444,31 +459,21 @@
         put(ak, h, nn(lanes(t, t), rows(hi, lo)))
         return carry
 
-    lax.fori_loop(0, heads, key_grads, 0)
+    each(0, heads, key_grads)
     k_total.start()
     q_total.turn()
     k_total.turn()
 
-    loss_seq[me] = loss_row[...]
-    peers(n, lambda i: loss_rows(me, lax.rem(me + i, n)).wait_recv())
-    total = lax.fori_loop(0, n, lambda i, t: t + loss_seq[i], jnp.zeros((8, 128), F32))
-    loss_ref[...] = jnp.broadcast_to(jnp.sum(total) * inv_total, (8, 128))
-
-    def unpack(src, dst):
-        for h in range(half):
-            x = src[h * 128 : (h + 1) * 128]
-            dst[h] = x[:, 0:64]
-            dst[h + half] = pltpu.roll(x, 64, 1)[:, 0:64]
+    loss_kv[col] = loss_row[...]
+    peers(m, lambda i: loss_cols(col, lax.rem(col + i, m)).wait_recv())
+    total = lax.fori_loop(0, m, lambda i, t: t + loss_kv[i], jnp.zeros((8, 128), F32))
+    loss_ref[0, 0] = jnp.sum(total) * inv_total
 
     q_total.finish()
-    unpack(aq_out, gq_ref)
-    k_total.finish()
-    unpack(ak_out, gk_ref)
+    gq_ref[...] = aq_out[...]
 
     fwd.drain()
     bwd.drain()
-    q_total.drain()
-    k_total.drain()
 
     @pl.when(me < n - 1)
     def _():
@@ -476,7 +481,11 @@
         edge_copy(1, me + 1).wait_send()
 
     peers(m, lambda i: loss_cols(lax.rem(col + i, m), col).wait_send())
-    peers(n, lambda i: loss_rows(lax.rem(me + i, n), me).wait_send())
+    save_y.wait()
+    k_total.finish()
+    gk_ref[...] = ak_out[...]
+    q_total.drain()
+    k_total.drain()
 
 
 def body(queries, keys, values, teacher, q_map, k_map):
@@ -489,26 +498,27 @@
     grad = heads * 64
     scan_bufs = lambda: [
         vmem((state, 128)),
-        vmem((8, 128)),
+        vmem((16, 128)),
         vmem((n, state // n, 128)),
         vmem((n, state // n, 128)),
         vmem((state, 128)),
-        vmem((n, 8, 128)),
-        vmem((n, 8, 128)),
-        vmem((8, 128)),
+        vmem((n, 16, 128)),
+        vmem((n, 16, 128)),
+        vmem((16, 128)),
     ]
     total_bufs = lambda: [vmem((grad, 128)), vmem((n, grad // n, 128)), vmem((grad // n, 128)), vmem((grad, 128))]
     spec = pl.BlockSpec(memory_space=pltpu.VMEM)
+    hbm = pl.BlockSpec(memory_space=pl.ANY)
     outs, grad_q, grad_k, loss = pl.pallas_call(
         functools.partial(kernel, n, m, heads, tok, width**-0.5, 1.0 / (tok * n)),
         out_shape=(
             jax.ShapeDtypeStruct((tok * heads, width), BF16),
-            jax.ShapeDtypeStruct(q_map.shape, F32),
-            jax.ShapeDtypeStruct(k_map.shape, F32),
-            jax.ShapeDtypeStruct((8, 128), F32),
+            jax.ShapeDtypeStruct((grad, width), F32),
+            jax.ShapeDtypeStruct((grad, width), F32),
+            jax.ShapeDtypeStruct((1, 1), F32),
         ),
-        in_specs=[spec] * 6,
-        out_specs=(spec,) * 4,
+        in_specs=[hbm, spec, spec, hbm, spec, spec],
+        out_specs=(hbm, spec, spec, pl.BlockSpec(memory_space=pltpu.SMEM)),
         scratch_shapes=[
             vmem((tok * heads, width)),
             vmem((tok + 2 * WIN, 128), BF16),
@@ -535,17 +545,18 @@
             *total_bufs(),
             vmem((8, 128)),
             vmem((m, 8, 128)),
-            vmem((8, 128)),
-            vmem((n, 8, 128)),
-            dma(4, n),
-            dma(3, n),
-            dma(4, n),
-            dma(3, n),
-            dma(4, n),
-            dma(4, n),
+            vmem((tok * heads, width), BF16),
+            vmem((tok * heads, width), BF16),
+            vmem((tok * heads, width), BF16),
+            dma(4),
+            dma(4),
+            dma(4),
+            dma(4),
+            dma(4),
+            dma(4),
             dma(2, 2),
             dma(2, m),
-            dma(2, n),
+            dma(3),
         ],
         compiler_params=pltpu.CompilerParams(collective_id=1, has_side_effects=True, vmem_limit_bytes=58 << 20),
     )(
@@ -553,10 +564,11 @@
         keys.reshape(tok, width),
         values.reshape(tok, width),
         teacher.reshape(tok * heads, width),
-        q_map,
-        k_map,
+        jnp.swapaxes(q_map, 1, 2),
+        jnp.swapaxes(k_map, 1, 2),
     )
-    return outs.reshape(tok, heads, width), grad_q, grad_k, loss[0, 0]
+    unmap = lambda g: jnp.swapaxes(g.reshape(heads, 64, width), 1, 2)
+    return outs.reshape(tok, heads, width), unmap(grad_q), unmap(grad_k), loss.reshape(())
 
 
 def solution(mesh):

time: 127 us -> 114 us (0.90)
  Pallas kernels: 117 us -> 107 us
  local copies, waits for them, and re-layouts: 8.74 us -> 4.05 us
  between operations: 0.66 us -> 2.41 us
    pallas_call x1, Pallas kernels: 117 us -> 107 us  [body(): pl.pallas_call(functools.partial(kernel, n, m, heads, tok, width ** (-0.5...]
    unnamed x9 -> x7, local copies, waits for them, and re-layouts: 7.46 us -> 4.05 us
    slice x1 -> x0, local copies, waits for them, and re-layouts: 1.27 us -> none  [body(): return (outs.reshape(tok, heads, width), grad_q, grad_k, loss[0, 0])]
where the time goes in v2:
time: 114 us
  Pallas kernels  107 us (94%)
  local copies, waits for them, and re-layouts  4.05 us (4%)
  between operations  2.41 us (2%)
    pallas_call x1, Pallas kernels, body(): pl.pallas_call(functools.partial(kernel, n, m, heads, tok, width ** (-0.5...  107 us
    unnamed x7, local copies, waits for them, and re-layouts  4.05 us

profile of v2, /device:TPU:6, one launch (start us, length us, event | category | flops | bytes accessed | tf_op | source)
XLA Modules:
  0.0 113.5 jit_solution(17772508522437857082)
XLA Ops:
  0.6 107.1 %shard_map.93 = (bf16[4096,128]{1,0:T(8,128)(2,1)}, f32[512,128]{1,0:T(8,128)}, f32[512,128]{1,0:T(8,128)}, f32[1,1]{1,0:T(1,128)}) custom-call(bf16[4096,128]{1,0:T(8,128)(2,1)} %bitcast.14, bf16[512,128]{1,0:T(8,128)(2,1)} %bitcast.19, bf16[512,128]{1,0:T(8,128)(2,1)} %bitcast.20, bf16[4096,128]{1,0:T(8,128)(2,1)} %bitcast.15, ...), custom_call_target="tpu_custom_call" | custom-call | tf_op jit(solution)/shard_map/pallas_call | solution.py:512
  107.7 0.0 copy-start.1
  107.7 2.3 %copy.14 = bf16[512,8,128]{2,1,0:T(8,128)(2,1)} copy(bf16[512,8,128]{2,1,0:T(8,128)(2,1)} %bitcast.16) | data formatting | bytes 2097152
  110.0 0.0 copy-done.1
  110.0 0.0 copy-start
  110.0 0.7 copy.15
  110.7 0.3 copy-done
  111.1 0.7 copy.16
Async XLA Ops:
  107.7 2.3 %copy-start.1 = (f32[512,128]{1,0:T(8,128)S(1)}, f32[512,128]{1,0:T(8,128)}, u32[]{:S(2)}) copy-start(f32[512,128]{1,0:T(8,128)} %get-tuple-element.9) | copy-start | bytes 786436
  110.0 1.0 copy-start

commit v3 on v2

--- a/solution.py
+++ b/solution.py
@@ -49,10 +49,9 @@
 
 
 class Scan:
-    def __init__(self, n, me, own, own_norm, got, part, out, got_norm, part_norm, out_norm, sems, norm_sems, reverse):
+    def __init__(self, n, me, own, own_norm, got, part, out, got_norm, part_norm, out_norm, sems, norm_sems, reverse, keeper):
         self.__dict__.update(locals())
         self.chunk = own.shape[0] // n
-        self.keeper = n // 2
 
     def piece(self, dev):
         return pl.ds(pl.multiple_of(dev * self.chunk, 8), self.chunk)
@@ -194,16 +193,17 @@
 
 def kernel(n, m, heads, tok, scale, inv_total, q_hbm, k_ref, v_ref, t_hbm, wq_ref, wk_ref,
            y_hbm, gq_ref, gk_ref, loss_ref,
-           tmp, kext, vext, vaug, vaugt, kt, qh, pqh, pql, pkh, pkl,
-           s_own, s_norm, s_got, s_part, s_in, sn_got, sn_part, sn_in,
+           tmp, kext, vext, vaug, vaugt, kt, qh, qt, pqh, pql, pkh, pkl,
+           bufs_fa, bufs_fb,
            loc, loc_norm, numer, gn_s, gd_s, dblk, dblk_norm,
-           d_own, d_norm, d_got, d_part, d_in, dn_got, dn_part, dn_in,
+           bufs_ba, bufs_bb,
            gkf, aq, aq_got, aq_part, aq_out, ak, ak_got, ak_part, ak_out,
            loss_row, loss_kv, q_ref, t_ref, y_ref,
-           f_sems, fn_sems, b_sems, bn_sems, q_sems, k_sems, e_sems, lk_sems, io_sems):
+           sems_fa, sems_fb, sems_ba, sems_bb, q_sems, k_sems, e_sems, lk_sems, io_sems):
     me = lax.axis_index("seq")
     col = lax.axis_index("kvh")
     nblk = tok // BLK
+    half = heads // 2
 
     barrier = pltpu.get_barrier_semaphore()
     peers(n, lambda i: pl.semaphore_signal(barrier, inc=1, device_id={"seq": lax.rem(me + i, n)}, device_id_type=MESH))
@@ -239,22 +239,55 @@
     def back(phi, g):
         return phi * (g - half_sums(phi * g))
 
+    fwd_a = Scan(n, me, *bufs_fa, *sems_fa, False, n // 2)
+    fwd_b = Scan(n, me, *bufs_fb, *sems_fb, False, n // 2 - 1)
+    bwd_a = Scan(n, me, *bufs_ba, *sems_ba, True, n // 2)
+    bwd_b = Scan(n, me, *bufs_bb, *sems_bb, True, n // 2 - 1)
+
+    def tile(h):
+        return pl.ds(pl.multiple_of(lax.rem(h, half) * 128, 128), 128)
+
+    def line(h):
+        return pl.ds(lax.rem(h, half), 1)
+
     kext[WIN : WIN + tok] = k_ref[...]
     vext[WIN : WIN + tok] = v_ref[...]
     vt = v_ref[...].astype(F32).T.astype(BF16)
     vt2 = lanes(vt, vt)
 
-    def own_keys(h, carry):
-        phi = maps(k_ref[...], wk_ref[h])
-        hi, lo = split(phi)
-        pkh[h, WIN : WIN + tok] = hi
-        pkl[h, WIN : WIN + tok] = lo
-        s_own[pl.ds(pl.multiple_of(h * 128, 128), 128)] = nn(vt2, rows(hi, lo))
-        s_norm[pl.ds(h, 1)] = jnp.sum(phi, axis=0, keepdims=True)
+    def own_keys(scan):
+        def own_keys(h, carry):
+            phi = maps(k_ref[...], wk_ref[h])
+            hi, lo = split(phi)
+            pkh[h, WIN : WIN + tok] = hi
+            pkl[h, WIN : WIN + tok] = lo
+            scan.own[tile(h)] = nn(vt2, rows(hi, lo))
+            scan.own_norm[line(h)] = jnp.sum(phi, axis=0, keepdims=True)
+            return carry
+
+        return own_keys
+
+    fwd_a.own_norm[...] = jnp.zeros((16, 128), F32)
+    fwd_b.own_norm[...] = jnp.zeros((16, 128), F32)
+    bwd_a.own_norm[...] = jnp.zeros((16, 128), F32)
+    bwd_b.own_norm[...] = jnp.zeros((16, 128), F32)
+    each(0, half, own_keys(fwd_a))
+    each(half, heads, own_keys(fwd_b))
+
+    load_q.wait()
+    tmp[...] = q_ref[...].astype(F32)
+
+    def query_maps(h, carry):
+        f = tmp[pl.ds(h, tok, stride=heads), :]
+        x = f.astype(BF16)
+        qh[h] = x
+        qt[h] = f.T.astype(BF16)
+        hi, lo = split(maps(x, wq_ref[h]))
+        pqh[h] = hi
+        pql[h] = lo
         return carry
 
-    each(0, heads, own_keys)
-    s_norm[8:16] = jnp.zeros((8, 128), F32)
+    each(0, heads, query_maps)
     pl.semaphore_wait(barrier, n - 1 + m - 1)
 
     def edge_copy(i, dev):
@@ -266,22 +299,9 @@
         edge_copy(0, me + 1).start()
         edge_copy(1, me + 1).start()
 
-    fwd = Scan(n, me, s_own, s_norm, s_got, s_part, s_in, sn_got, sn_part, sn_in, f_sems, fn_sems, False)
-    bwd = Scan(n, me, d_own, d_norm, d_got, d_part, d_in, dn_got, dn_part, dn_in, b_sems, bn_sems, True)
-    fwd.start()
-
-    load_q.wait()
-    tmp[...] = q_ref[...].astype(F32)
-
-    def query_maps(h, carry):
-        x = tmp[pl.ds(h, tok, stride=heads), :].astype(BF16)
-        qh[h] = x
-        hi, lo = split(maps(x, wq_ref[h]))
-        pqh[h] = hi
-        pql[h] = lo
-        return carry
-
-    each(0, heads, query_maps)
+
+    fwd_a.start()
+    fwd_b.start()
 
     @pl.when(me == 0)
     def _():
@@ -351,17 +371,18 @@
                 state = state + nn(lanes(vb, vb), rows(kh, kl))
         return carry
 
-    each(0, heads // 2, local_forward)
-    fwd.turn()
-    each(heads // 2, heads, local_forward)
-    fwd.finish()
+    each(0, half, local_forward)
+    fwd_a.turn()
+    each(half, half + 2, local_forward)
+    fwd_b.turn()
+    each(half + 2, heads, local_forward)
 
     load_t.wait()
     tmp[...] = t_ref[...].astype(F32)
 
-    def outputs(h, squares):
-        prior = s_in[pl.ds(pl.multiple_of(h * 128, 128), 128)]
-        prior_norm = jnp.broadcast_to(sn_in[pl.ds(h, 1)], (128, 128))
+    def outputs(h, squares, fwd, bwd):
+        prior = fwd.out[tile(h)]
+        prior_norm = jnp.broadcast_to(fwd.out_norm[line(h)], (128, 128))
         shi, slo = split(rows(prior, prior_norm))
         s3 = lanes(shi, shi, slo)
         d_sum = jnp.zeros((128, 128), F32)
@@ -388,12 +409,17 @@
             dblk_norm[h, b] = jnp.broadcast_to(dn, (8, 128))
             d_sum = d_sum + d
             dn_sum = dn_sum + dn
-        d_own[pl.ds(pl.multiple_of(h * 128, 128), 128)] = d_sum
-        d_norm[pl.ds(h, 1)] = dn_sum
+        bwd.own[tile(h)] = d_sum
+        bwd.own_norm[line(h)] = dn_sum
         return squares
 
-    d_norm[8:16] = each(0, heads, outputs, jnp.zeros((8, 128), F32))
-    bwd.start()
+    def half_outputs(lo, fwd, bwd):
+        fwd.finish()
+        bwd.own_norm[8:16] = each(lo, lo + half, lambda h, c: outputs(h, c, fwd, bwd), jnp.zeros((8, 128), F32))
+        bwd.start()
+
+    half_outputs(0, fwd_a, bwd_a)
+    half_outputs(half, fwd_b, bwd_b)
 
     def loss_cols(dev, src):
         return remote(loss_row, loss_kv.at[src], lk_sems.at[0, dev], lk_sems.at[1, src], dev, "kvh")
@@ -401,9 +427,9 @@
     y_ref[...] = tmp[...].astype(BF16)
     save_y.start()
 
-    def local_backward(h, carry):
-        prior = s_in[pl.ds(pl.multiple_of(h * 128, 128), 128)]
-        prior_norm = sn_in[pl.ds(h, 1)]
+    def local_backward(h, carry, fwd):
+        prior = fwd.out[tile(h)]
+        prior_norm = fwd.out_norm[line(h)]
         later = jnp.zeros((128, 128), F32)
         later_norm = jnp.zeros((1, 128), F32)
         g = jnp.zeros((128, 128), F32)
@@ -423,8 +449,8 @@
             norm = prior_norm + loc_norm[h, b, 0:1]
             gqf = nn(lanes(fhi, flo, fhi, ghi, glo, ghi), rows(kh, kh, kl, shi, shi, slo)) + gd * norm
             rhi, rlo = split(back(qhi.astype(F32) + qlo.astype(F32), gqf))
-            qt = qh[h, at : at + BLK].astype(F32).T.astype(BF16)
-            g = g + nn(lanes(qt, qt), rows(rhi, rlo))
+            qtb = qt[h, :, at : at + BLK]
+            g = g + nn(lanes(qtb, qtb), rows(rhi, rlo))
             thi, tlo = split(gf.T)
             lhi, llo = split(later)
             gkf[h, at : at + BLK] = (
@@ -439,27 +465,36 @@
         g = g.T
         ref[pl.ds(pl.multiple_of(h * 64, 64), 64)] = g[0:64] - g[64:128]
 
-    each(0, heads // 2, local_backward)
-    bwd.turn()
-    each(heads // 2, heads, local_backward)
+    def backward_a(h, carry):
+        return local_backward(h, carry, fwd_a)
+
+    def backward_b(h, carry):
+        return local_backward(h, carry, fwd_b)
+
+    each(0, 2, backward_a)
+    bwd_a.turn()
+    each(2, half, backward_a)
+    bwd_b.turn()
+    each(half, heads, backward_b)
     q_total = Total(n, me, aq, aq_got, aq_part, aq_out, q_sems)
     k_total = Total(n, me, ak, ak_got, ak_part, ak_out, k_sems)
     q_total.start()
-    bwd.finish()
-    loss_row[...] = dn_in[8:16]
-    peers(m, lambda i: loss_cols(lax.rem(col + i, m), col).start())
-
-    def key_grads(h, carry):
-        shi, slo = split(d_in[pl.ds(pl.multiple_of(h * 128, 128), 128)])
-        suffix_norm = dn_in[pl.ds(h, 1)]
+
+    def key_grads(h, carry, bwd):
+        shi, slo = split(bwd.out[tile(h)])
         v = vext[0:tok]
-        g = gkf[h] + nn(lanes(v, v), rows(shi, slo)) + suffix_norm
+        g = gkf[h] + nn(lanes(v, v), rows(shi, slo)) + bwd.out_norm[line(h)]
         hi, lo = split(back(pkh[h, 0:tok].astype(F32) + pkl[h, 0:tok].astype(F32), g))
         t = kt[...]
         put(ak, h, nn(lanes(t, t), rows(hi, lo)))
         return carry
 
-    each(0, heads, key_grads)
+    bwd_a.finish()
+    each(0, half, lambda h, c: key_grads(h, c, bwd_a))
+    bwd_b.finish()
+    loss_row[...] = bwd_a.out_norm[8:16] + bwd_b.out_norm[8:16]
+    peers(m, lambda i: loss_cols(lax.rem(col + i, m), col).start())
+    each(half, heads, lambda h, c: key_grads(h, c, bwd_b))
     k_total.start()
     q_total.turn()
     k_total.turn()
@@ -472,8 +507,10 @@
     q_total.finish()
     gq_ref[...] = aq_out[...]
 
-    fwd.drain()
-    bwd.drain()
+    fwd_a.drain()
+    fwd_b.drain()
+    bwd_a.drain()
+    bwd_b.drain()
 
     @pl.when(me < n - 1)
     def _():
@@ -494,7 +531,7 @@
     nblk = tok // BLK
     vmem = lambda shape, dtype=F32: pltpu.VMEM(shape, dtype)
     dma = lambda *shape: pltpu.SemaphoreType.DMA(shape)
-    state = heads * 128
+    state = heads // 2 * 128
     grad = heads * 64
     scan_bufs = lambda: [
         vmem((state, 128)),
@@ -527,11 +564,13 @@
             vmem((256, tok), BF16),
             vmem((128, tok), BF16),
             vmem((heads, tok, 128), BF16),
+            vmem((heads, 128, tok), BF16),
             vmem((heads, tok, 128), BF16),
             vmem((heads, tok, 128), BF16),
             vmem((heads, tok + WIN, 128), BF16),
             vmem((heads, tok + WIN, 128), BF16),
-            *scan_bufs(),
+            scan_bufs(),
+            scan_bufs(),
             vmem((heads, nblk, 128, 128)),
             vmem((heads, nblk, 8, 128)),
             vmem((heads, tok, 256)),
@@ -539,7 +578,8 @@
             vmem((heads, tok, 128)),
             vmem((heads, nblk, 128, 128)),
             vmem((heads, nblk, 8, 128)),
-            *scan_bufs(),
+            scan_bufs(),
+            scan_bufs(),
             vmem((heads, tok, 128)),
             *total_bufs(),
             *total_bufs(),
@@ -548,10 +588,10 @@
             vmem((tok * heads, width), BF16),
             vmem((tok * heads, width), BF16),
             vmem((tok * heads, width), BF16),
-            dma(4),
-            dma(4),
-            dma(4),
-            dma(4),
+            (dma(4), dma(4)),
+            (dma(4), dma(4)),
+            (dma(4), dma(4)),
+            (dma(4), dma(4)),
             dma(4),
             dma(4),
             dma(2, 2),

time: 114 us -> 103 us (0.904)
  Pallas kernels: 107 us -> 96.4 us
    pallas_call x1, Pallas kernels: 107 us -> 96.4 us  [body(): pl.pallas_call(functools.partial(kernel, n, m, heads, tok, width ** (-0.5...]
where the time goes in v3:
time: 103 us
  Pallas kernels  96.4 us (94%)
  local copies, waits for them, and re-layouts  4.05 us (4%)
  between operations  2.41 us (2%)
    pallas_call x1, Pallas kernels, body(): pl.pallas_call(functools.partial(kernel, n, m, heads, tok, width ** (-0.5...  96.4 us
    unnamed x7, local copies, waits for them, and re-layouts  4.05 us

profile of v3, /device:TPU:6, one launch (start us, length us, event | category | flops | bytes accessed | tf_op | source)
XLA Modules:
  0.0 102.9 jit_solution(15978118733939804356)
XLA Ops:
  0.6 96.4 %shard_map.93 = (bf16[4096,128]{1,0:T(8,128)(2,1)}, f32[512,128]{1,0:T(8,128)}, f32[512,128]{1,0:T(8,128)}, f32[1,1]{1,0:T(1,128)}) custom-call(bf16[4096,128]{1,0:T(8,128)(2,1)} %bitcast.14, bf16[512,128]{1,0:T(8,128)(2,1)} %bitcast.19, bf16[512,128]{1,0:T(8,128)(2,1)} %bitcast.20, bf16[4096,128]{1,0:T(8,128)(2,1)} %bitcast.15, ...), custom_call_target="tpu_custom_call" | custom-call | tf_op jit(solution)/shard_map/pallas_call | solution.py:549
  97.1 0.0 copy-start.1
  97.1 2.3 %copy.14 = bf16[512,8,128]{2,1,0:T(8,128)(2,1)} copy(bf16[512,8,128]{2,1,0:T(8,128)(2,1)} %bitcast.16) | data formatting | bytes 2097152
  99.4 0.0 copy-done.1
  99.4 0.0 copy-start
  99.4 0.7 copy.15
  100.1 0.3 copy-done
  100.4 0.7 copy.16
Async XLA Ops:
  97.1 2.3 %copy-start.1 = (f32[512,128]{1,0:T(8,128)S(1)}, f32[512,128]{1,0:T(8,128)}, u32[]{:S(2)}) copy-start(f32[512,128]{1,0:T(8,128)} %get-tuple-element.9) | copy-start | bytes 786436
  99.4 1.0 %copy-start = (f32[512,128]{1,0:T(8,128)S(1)}, f32[512,128]{1,0:T(8,128)}, u32[]{:S(2)}) copy-start(f32[512,128]{1,0:T(8,128)} %get-tuple-element.10) | copy-start | bytes 786436

commit v4 on v3

--- a/solution.py
+++ b/solution.py
@@ -197,9 +197,9 @@
            bufs_fa, bufs_fb,
            loc, loc_norm, numer, gn_s, gd_s, dblk, dblk_norm,
            bufs_ba, bufs_bb,
-           gkf, aq, aq_got, aq_part, aq_out, ak, ak_got, ak_part, ak_out,
+           gkf, bufs_qa, bufs_qb, bufs_ka, bufs_kb,
            loss_row, loss_kv, q_ref, t_ref, y_ref,
-           sems_fa, sems_fb, sems_ba, sems_bb, q_sems, k_sems, e_sems, lk_sems, io_sems):
+           sems_fa, sems_fb, sems_ba, sems_bb, sems_qa, sems_qb, sems_ka, sems_kb, e_sems, lk_sems, io_sems):
     me = lax.axis_index("seq")
     col = lax.axis_index("kvh")
     nblk = tok // BLK
@@ -427,7 +427,7 @@
     y_ref[...] = tmp[...].astype(BF16)
     save_y.start()
 
-    def local_backward(h, carry, fwd):
+    def local_backward(h, carry, fwd, into):
         prior = fwd.out[tile(h)]
         prior_norm = fwd.out_norm[line(h)]
         later = jnp.zeros((128, 128), F32)
@@ -458,54 +458,64 @@
             )
             later = later + dblk[h, b]
             later_norm = later_norm + dblk_norm[h, b, 0:1]
-        put(aq, h, g)
+        put(into, h, g)
         return carry
 
     def put(ref, h, g):
         g = g.T
-        ref[pl.ds(pl.multiple_of(h * 64, 64), 64)] = g[0:64] - g[64:128]
+        ref[pl.ds(pl.multiple_of(lax.rem(h, half) * 64, 64), 64)] = g[0:64] - g[64:128]
+
+    q_a = Total(n, me, *bufs_qa, sems_qa)
+    q_b = Total(n, me, *bufs_qb, sems_qb)
+    k_a = Total(n, me, *bufs_ka, sems_ka)
+    k_b = Total(n, me, *bufs_kb, sems_kb)
 
     def backward_a(h, carry):
-        return local_backward(h, carry, fwd_a)
+        return local_backward(h, carry, fwd_a, q_a.own)
 
     def backward_b(h, carry):
-        return local_backward(h, carry, fwd_b)
+        return local_backward(h, carry, fwd_b, q_b.own)
 
     each(0, 2, backward_a)
     bwd_a.turn()
     each(2, half, backward_a)
     bwd_b.turn()
+    q_a.start()
     each(half, heads, backward_b)
-    q_total = Total(n, me, aq, aq_got, aq_part, aq_out, q_sems)
-    k_total = Total(n, me, ak, ak_got, ak_part, ak_out, k_sems)
-    q_total.start()
-
-    def key_grads(h, carry, bwd):
+    q_b.start()
+    q_a.turn()
+
+    def key_grads(h, carry, bwd, into):
         shi, slo = split(bwd.out[tile(h)])
         v = vext[0:tok]
         g = gkf[h] + nn(lanes(v, v), rows(shi, slo)) + bwd.out_norm[line(h)]
         hi, lo = split(back(pkh[h, 0:tok].astype(F32) + pkl[h, 0:tok].astype(F32), g))
         t = kt[...]
-        put(ak, h, nn(lanes(t, t), rows(hi, lo)))
+        put(into, h, nn(lanes(t, t), rows(hi, lo)))
         return carry
 
     bwd_a.finish()
-    each(0, half, lambda h, c: key_grads(h, c, bwd_a))
+    each(0, half, lambda h, c: key_grads(h, c, bwd_a, k_a.own))
+    k_a.start()
     bwd_b.finish()
     loss_row[...] = bwd_a.out_norm[8:16] + bwd_b.out_norm[8:16]
     peers(m, lambda i: loss_cols(lax.rem(col + i, m), col).start())
-    each(half, heads, lambda h, c: key_grads(h, c, bwd_b))
-    k_total.start()
-    q_total.turn()
-    k_total.turn()
+    each(half, heads, lambda h, c: key_grads(h, c, bwd_b, k_b.own))
+    k_b.start()
+    q_b.turn()
+    k_a.turn()
+    k_b.turn()
 
     loss_kv[col] = loss_row[...]
     peers(m, lambda i: loss_cols(col, lax.rem(col + i, m)).wait_recv())
     total = lax.fori_loop(0, m, lambda i, t: t + loss_kv[i], jnp.zeros((8, 128), F32))
     loss_ref[0, 0] = jnp.sum(total) * inv_total
 
-    q_total.finish()
-    gq_ref[...] = aq_out[...]
+    cut = half * 64
+    q_a.finish()
+    gq_ref[0:cut] = q_a.out[...]
+    q_b.finish()
+    gq_ref[cut:] = q_b.out[...]
 
     fwd_a.drain()
     fwd_b.drain()
@@ -519,10 +529,14 @@
 
     peers(m, lambda i: loss_cols(lax.rem(col + i, m), col).wait_send())
     save_y.wait()
-    k_total.finish()
-    gk_ref[...] = ak_out[...]
-    q_total.drain()
-    k_total.drain()
+    q_a.drain()
+    q_b.drain()
+    k_a.finish()
+    gk_ref[0:cut] = k_a.out[...]
+    k_b.finish()
+    gk_ref[cut:] = k_b.out[...]
+    k_a.drain()
+    k_b.drain()
 
 
 def body(queries, keys, values, teacher, q_map, k_map):
@@ -543,7 +557,8 @@
         vmem((n, 16, 128)),
         vmem((16, 128)),
     ]
-    total_bufs = lambda: [vmem((grad, 128)), vmem((n, grad // n, 128)), vmem((grad // n, 128)), vmem((grad, 128))]
+    part = grad // 2
+    total_bufs = lambda: [vmem((part, 128)), vmem((n, part // n, 128)), vmem((part // n, 128)), vmem((part, 128))]
     spec = pl.BlockSpec(memory_space=pltpu.VMEM)
     hbm = pl.BlockSpec(memory_space=pl.ANY)
     outs, grad_q, grad_k, loss = pl.pallas_call(
@@ -581,8 +596,10 @@
             scan_bufs(),
             scan_bufs(),
             vmem((heads, tok, 128)),
-            *total_bufs(),
-            *total_bufs(),
+            total_bufs(),
+            total_bufs(),
+            total_bufs(),
+            total_bufs(),
             vmem((8, 128)),
             vmem((m, 8, 128)),
             vmem((tok * heads, width), BF16),
@@ -592,6 +609,8 @@
             (dma(4), dma(4)),
             (dma(4), dma(4)),
             (dma(4), dma(4)),
+            dma(4),
+            dma(4),
             dma(4),
             dma(4),
             dma(2, 2),

time: 103 us -> 104 us (level)
  no operation moved by 1% of the time
where the time goes in v4:
time: 104 us; the launch traced here: 103 us
  Pallas kernels  96.8 us (93%)
  local copies, waits for them, and re-layouts  4.05 us (4%)
  between operations  2.41 us (2%)
    pallas_call x1, Pallas kernels, body(): pl.pallas_call(functools.partial(kernel, n, m, heads, tok, width ** (-0.5...  96.8 us
    unnamed x7, local copies, waits for them, and re-layouts  4.05 us

profile of v4, /device:TPU:6, one launch (start us, length us, event | category | flops | bytes accessed | tf_op | source)
XLA Modules:
  0.0 103.2 jit_solution(4863379862302402023)
XLA Ops:
  0.6 96.8 %shard_map.93 = (bf16[4096,128]{1,0:T(8,128)(2,1)}, f32[512,128]{1,0:T(8,128)}, f32[512,128]{1,0:T(8,128)}, f32[1,1]{1,0:T(1,128)}) custom-call(bf16[4096,128]{1,0:T(8,128)(2,1)} %bitcast.14, bf16[512,128]{1,0:T(8,128)(2,1)} %bitcast.19, bf16[512,128]{1,0:T(8,128)(2,1)} %bitcast.20, bf16[4096,128]{1,0:T(8,128)(2,1)} %bitcast.15, ...), custom_call_target="tpu_custom_call" | custom-call | tf_op jit(solution)/shard_map/pallas_call | solution.py:564
  97.4 0.0 copy-start.1
  97.4 2.3 %copy.14 = bf16[512,8,128]{2,1,0:T(8,128)(2,1)} copy(bf16[512,8,128]{2,1,0:T(8,128)(2,1)} %bitcast.16) | data formatting | bytes 2097152
  99.7 0.0 copy-done.1
  99.7 0.0 copy-start
  99.7 0.7 copy.15
  100.4 0.3 copy-done
  100.8 0.7 copy.16
Async XLA Ops:
  97.4 2.3 %copy-start.1 = (f32[512,128]{1,0:T(8,128)S(1)}, f32[512,128]{1,0:T(8,128)}, u32[]{:S(2)}) copy-start(f32[512,128]{1,0:T(8,128)} %get-tuple-element.9) | copy-start | bytes 786436
  99.7 1.0 %copy-start = (f32[512,128]{1,0:T(8,128)S(1)}, f32[512,128]{1,0:T(8,128)}, u32[]{:S(2)}) copy-start(f32[512,128]{1,0:T(8,128)} %get-tuple-element.10) | copy-start | bytes 786436

commit v5 on v3

--- a/solution.py
+++ b/solution.py
@@ -371,7 +371,7 @@
                 state = state + nn(lanes(vb, vb), rows(kh, kl))
         return carry
 
-    each(0, half, local_forward)
+    each(0, half, local_forward, unroll=4)
     fwd_a.turn()
     each(half, half + 2, local_forward)
     fwd_b.turn()
@@ -415,7 +415,7 @@
 
     def half_outputs(lo, fwd, bwd):
         fwd.finish()
-        bwd.own_norm[8:16] = each(lo, lo + half, lambda h, c: outputs(h, c, fwd, bwd), jnp.zeros((8, 128), F32))
+        bwd.own_norm[8:16] = each(lo, lo + half, lambda h, c: outputs(h, c, fwd, bwd), jnp.zeros((8, 128), F32), 4)
         bwd.start()
 
     half_outputs(0, fwd_a, bwd_a)
@@ -475,7 +475,7 @@
     bwd_a.turn()
     each(2, half, backward_a)
     bwd_b.turn()
-    each(half, heads, backward_b)
+    each(half, heads, backward_b, unroll=4)
     q_total = Total(n, me, aq, aq_got, aq_part, aq_out, q_sems)
     k_total = Total(n, me, ak, ak_got, ak_part, ak_out, k_sems)
     q_total.start()

time: 103 us -> 99.8 us (0.969)
  Pallas kernels: 96.4 us -> 93.1 us
    pallas_call x1, Pallas kernels: 96.4 us -> 93.1 us  [body(): pl.pallas_call(functools.partial(kernel, n, m, heads, tok, width ** (-0.5...]
where the time goes in v5:
time: 99.8 us; the launch traced here: 99.6 us
  Pallas kernels  93.1 us (93%)
  local copies, waits for them, and re-layouts  4.05 us (4%)
  between operations  2.41 us (2%)
    pallas_call x1, Pallas kernels, body(): pl.pallas_call(functools.partial(kernel, n, m, heads, tok, width ** (-0.5...  93.1 us
    unnamed x7, local copies, waits for them, and re-layouts  4.05 us

profile of v5, /device:TPU:6, one launch (start us, length us, event | category | flops | bytes accessed | tf_op | source)
XLA Modules:
  0.0 99.6 jit_solution(11336351554031141960)
XLA Ops:
  0.6 93.1 %shard_map.93 = (bf16[4096,128]{1,0:T(8,128)(2,1)}, f32[512,128]{1,0:T(8,128)}, f32[512,128]{1,0:T(8,128)}, f32[1,1]{1,0:T(1,128)}) custom-call(bf16[4096,128]{1,0:T(8,128)(2,1)} %bitcast.14, bf16[512,128]{1,0:T(8,128)(2,1)} %bitcast.19, bf16[512,128]{1,0:T(8,128)(2,1)} %bitcast.20, bf16[4096,128]{1,0:T(8,128)(2,1)} %bitcast.15, ...), custom_call_target="tpu_custom_call" | custom-call | tf_op jit(solution)/shard_map/pallas_call | solution.py:549
  93.8 0.0 copy-start.1
  93.8 2.3 %copy.14 = bf16[512,8,128]{2,1,0:T(8,128)(2,1)} copy(bf16[512,8,128]{2,1,0:T(8,128)(2,1)} %bitcast.16) | data formatting | bytes 2097152
  96.1 0.0 copy-done.1
  96.1 0.0 copy-start
  96.1 0.7 copy.15
  96.8 0.3 copy-done
  97.1 0.7 copy.16
Async XLA Ops:
  93.8 2.3 %copy-start.1 = (f32[512,128]{1,0:T(8,128)S(1)}, f32[512,128]{1,0:T(8,128)}, u32[]{:S(2)}) copy-start(f32[512,128]{1,0:T(8,128)} %get-tuple-element.9) | copy-start | bytes 786436
  96.1 1.0 %copy-start = (f32[512,128]{1,0:T(8,128)S(1)}, f32[512,128]{1,0:T(8,128)}, u32[]{:S(2)}) copy-start(f32[512,128]{1,0:T(8,128)} %get-tuple-element.10) | copy-start | bytes 786436
